TPU v7x, 128 devices: a whole 4x4x4 slice. The times are simulated.
128 devices in a mesh: dp: 4 (over x), context: 4 (over y), expert: 8 (over z, core).
Axes of the slice: x: 4, y: 4, z: 4, core: 2. Of those that a mesh axis runs over, the one named last changes fastest.
Arguments:
- tokens: bfloat16 [2, 4, 32, 192, 768], P(None, 'dp', ('context', 'expert')), may hold values from -6 to 6
- prior_logits: float32 [2, 4, 32, 192, 12], P(None, 'dp', ('context', 'expert')), may hold values from -3 to 3
- routes: int32 [2, 4, 32, 192, 2], P(None, 'dp', ('context', 'expert')), may hold values from 0 to 11, all different within a row; in each aligned block of 192 rows (0 to 191, 192 to 383, ..., all dimensions but the last counted through in order) at most 36 rows name the same one
- drops: int32 [2, 4, 32, 192, 2], P(None, 'dp', ('context', 'expert')), may hold values 0 or 1
- cont_lengths: int32 [2, 4, 32], P(None, 'dp', ('context', 'expert')), may hold values from 1 to 128, 3072 in all within a row
- norm_gain: bfloat16 [768], replicated, may hold values from 0.5 to 1.5
- w_query: bfloat16 [768, 768], replicated, may hold values from -0.21875 to 0.21875
- w_key: bfloat16 [768, 768], replicated, may hold values from -0.21875 to 0.21875
- w_value: bfloat16 [768, 768], replicated, may hold values from -0.21875 to 0.21875
- w_out: bfloat16 [768, 768], replicated, may hold values from -1.75 to 1.75
- ffn_gain: bfloat16 [768], replicated, may hold values from 0.5 to 1.5
- w_router: bfloat16 [768, 12], replicated, may hold values from -0.109375 to 0.109375
- w_const: bfloat16 [2, 768, 2], replicated, may hold values from -0.21875 to 0.21875
- const_vec: bfloat16 [2, 768], replicated, may hold values from -24 to 24
- w_gate: bfloat16 [8, 768, 2048], P('expert'), may hold values from -0.21875 to 0.21875
- w_up: bfloat16 [8, 768, 2048], P('expert'), may hold values from -0.21875 to 0.21875
- w_down: bfloat16 [8, 2048, 768], P('expert'), may hold values from -1 to 1
- out_grad: bfloat16 [2, 4, 32, 192, 768], P(None, 'dp', ('context', 'expert')), may hold values from -6 to 6
Outputs:
- mixed: bfloat16 [2, 4, 32, 192, 768], P(None, 'dp', ('context', 'expert'))
- tokens_grad: bfloat16 [2, 4, 32, 192, 768], P(None, 'dp', ('context', 'expert'))
- prior_grad: float32 [2, 4, 32, 192, 12], P(None, 'dp', ('context', 'expert'))
- norm_gain_grad: float32 [768], replicated
- w_query_grad: float32 [768, 768], replicated
- w_key_grad: float32 [768, 768], replicated
- w_value_grad: float32 [768, 768], replicated
- w_out_grad: float32 [768, 768], replicated
- ffn_gain_grad: float32 [768], replicated
- w_router_grad: float32 [768, 12], replicated
- w_const_grad: float32 [2, 768, 2], replicated
- const_vec_grad: float32 [2, 768], replicated
- w_gate_grad: float32 [8, 768, 2048], P('expert')
- w_up_grad: float32 [8, 768, 2048], P('expert')
- w_down_grad: float32 [8, 2048, 768], P('expert')
Inputs may be any that keep to these rules, and one draw needn't show every extreme that they name: Targets 0 to 7 are feed-forward experts, 8 the zero expert, 9 the copy expert, the rest constant experts; a token's routes differ; among the 192 rows of one slot of one micro-batch no target is named more than 36 times, a bound that some block reaches. 1 drops the route. `cont_lengths`: the 32 lengths of a group sum to 3072, and the longest is 128.
All inputs are finite; a program needn't handle non-finite values. No bound on the sum of `drops` on one device may be relied on, other than what follows from the above.
Results may differ from a plain program's by a relative error of at most 0.03.
Values may be sent and summed in bfloat16 or wider, within the bound.
No kernel may reach another device: no remote copies, remote signals or barrier semaphores. Data moves between devices by JAX's collectives and lax.ppermute only.
A program may use at most 320 MiB of HBM per device.

v0:
```python
import math

import jax
import jax.numpy as jnp
from jax import lax
from jax.sharding import PartitionSpec as P

HEADS = 12
HEAD_SIZE = 64
EXPERTS = 8
CONSTS = 2
TOP = 2
TARGETS = 12
CLEN = 128


highest = lax.Precision.HIGHEST
norm_eps = 1e-05
very_low = -1e30


def rms_scale(values_in, gain_vec):
    return (
        values_in
        * lax.rsqrt(jnp.mean(values_in * values_in, axis=-1, keepdims=True) + norm_eps)
        * gain_vec
    )


def mixture(two_float, router_w, prior_row, const_w, const_v, route_out, route_ids, active):
    logits = jnp.dot(two_float, router_w, precision=highest) + prior_row
    chances = jax.nn.softmax(logits, axis=-1)
    target_hot = (route_ids[..., None] == jnp.arange(TARGETS, dtype=jnp.int32)).astype(jnp.float32)
    route_gate = jnp.sum(target_hot * chances[..., None, :], axis=-1) * active.astype(jnp.float32)
    mixed_out = jnp.sum(route_gate[..., None] * route_out, axis=-2)
    copy_gate = jnp.sum(route_gate * (route_ids == EXPERTS + 1).astype(jnp.float32), axis=-1)
    mixed_out = mixed_out + copy_gate[..., None] * two_float
    for const_index in range(CONSTS):
        shares = jax.nn.softmax(
            jnp.dot(two_float, const_w[const_index], precision=highest), axis=-1
        )
        const_gate = jnp.sum(
            route_gate * (route_ids == EXPERTS + 2 + const_index).astype(jnp.float32), axis=-1
        )
        mixed_out = mixed_out + const_gate[..., None] * (
            shares[..., 0:1] * two_float + shares[..., 1:2] * const_v[const_index]
        )
    return mixed_out


def fold_scores(state_in, queries, key_rows, value_rows, allowed, score_scale):
    row_max, row_sum, weighted = state_in
    scores = (
        jnp.einsum("qhd,khd->hqk", queries, key_rows, preferred_element_type=jnp.float32)
        * score_scale
    )
    scores = jnp.where(allowed[None], scores, very_low)
    new_max = jnp.maximum(row_max, jnp.max(scores, axis=-1))
    weights = jnp.where(allowed[None], jnp.exp(scores - new_max[..., None]), 0.0)
    factor = jnp.exp(row_max - new_max)
    row_sum = row_sum * factor + jnp.sum(weights, axis=-1)
    weighted = weighted * factor[..., None] + jnp.einsum(
        "hqk,khd->hqd", weights.astype(jnp.bfloat16), value_rows, preferred_element_type=jnp.float32
    )
    return (new_max, row_sum, weighted)


def score_grads(queries, key_rows, value_rows, allowed, log_norm, attn_grad_h, delta, score_scale):
    scores = (
        jnp.einsum("qhd,khd->hqk", queries, key_rows, preferred_element_type=jnp.float32)
        * score_scale
    )
    chances = jnp.where(allowed[None], jnp.exp(scores - log_norm[..., None]), 0.0)
    prob_low = chances.astype(jnp.bfloat16)
    prob_grad = jnp.einsum(
        "qhd,khd->hqk", attn_grad_h, value_rows, preferred_element_type=jnp.float32
    )
    score_grad = (chances * (prob_grad - delta[..., None])).astype(jnp.bfloat16)
    query_part = (
        jnp.einsum("hqk,khd->qhd", score_grad, key_rows, preferred_element_type=jnp.float32)
        * score_scale
    )
    key_part = (
        jnp.einsum("hqk,qhd->khd", score_grad, queries, preferred_element_type=jnp.float32)
        * score_scale
    )
    value_part = jnp.einsum(
        "hqk,qhd->khd", prob_low, attn_grad_h, preferred_element_type=jnp.float32
    )
    return (query_part, key_part, value_part)


def add_pair(left_in, right_in):
    return left_in + right_in


def on_device(
    tokens,
    prior_logits,
    routes,
    drops,
    cont_lengths,
    norm_gain,
    w_query,
    w_key,
    w_value,
    w_out,
    ffn_gain,
    w_router,
    w_const,
    const_vec,
    w_gate,
    w_up,
    w_down,
    out_grad,
):
    micro_count = tokens.shape[0]
    row_count = tokens.shape[3]
    model_width = tokens.shape[4]
    prompt_rows = row_count - CLEN
    capacity = row_count * 3 // 16
    group_width = lax.axis_size(("context", "expert"))
    slot_index = lax.axis_index(("context", "expert"))
    prompt_total = prompt_rows * group_width
    block_rows = math.gcd(prompt_total, 512)
    score_scale = 1.0 / math.sqrt(HEAD_SIZE)
    expert_group = lax.axis_size("expert")
    local_experts = w_gate.shape[0]
    gain_one = norm_gain.astype(jnp.float32)
    gain_two = ffn_gain.astype(jnp.float32)
    router_f = w_router.astype(jnp.float32)
    const_wf = w_const.astype(jnp.float32)
    const_vf = const_vec.astype(jnp.float32)
    row_ids = jnp.arange(row_count, dtype=jnp.int32)
    query_pos = jnp.where(row_ids < prompt_rows, slot_index * prompt_rows + row_ids, prompt_total)
    self_allowed = (
        (row_ids - prompt_rows)[:, None] >= jnp.arange(CLEN, dtype=jnp.int32)[None, :]
    ) & (row_ids >= prompt_rows)[:, None]
    slot_range = jnp.arange(EXPERTS * capacity, dtype=jnp.int32)
    dense_acc = (
        jnp.zeros_like(gain_one),
        jnp.zeros(w_query.shape, jnp.float32),
        jnp.zeros(w_key.shape, jnp.float32),
        jnp.zeros(w_value.shape, jnp.float32),
        jnp.zeros(w_out.shape, jnp.float32),
        jnp.zeros_like(gain_two),
        jnp.zeros_like(router_f),
        jnp.zeros_like(const_wf),
        jnp.zeros_like(const_vf),
    )
    expert_acc = (
        jnp.zeros(w_gate.shape, jnp.float32),
        jnp.zeros(w_up.shape, jnp.float32),
        jnp.zeros(w_down.shape, jnp.float32),
    )
    outputs_list = []
    token_grads = []
    prior_grads = []
    for micro in range(micro_count):
        x_rows = tokens[micro, 0, 0].astype(jnp.float32)
        prior_row = prior_logits[micro, 0, 0]
        route_ids = routes[micro, 0, 0]
        cont_len = cont_lengths[micro, 0, 0]
        row_live = (row_ids < prompt_rows + cont_len).astype(jnp.int32)
        active = (1 - drops[micro, 0, 0]) * row_live[:, None]
        normed = rms_scale(x_rows, gain_one).astype(jnp.bfloat16)
        queries = (
            jnp.dot(normed, w_query, preferred_element_type=jnp.float32)
            .astype(jnp.bfloat16)
            .reshape(row_count, HEADS, HEAD_SIZE)
        )
        key_all = (
            jnp.dot(normed, w_key, preferred_element_type=jnp.float32)
            .astype(jnp.bfloat16)
            .reshape(row_count, HEADS, HEAD_SIZE)
        )
        value_all = (
            jnp.dot(normed, w_value, preferred_element_type=jnp.float32)
            .astype(jnp.bfloat16)
            .reshape(row_count, HEADS, HEAD_SIZE)
        )
        prompt_keys = key_all[:prompt_rows]
        prompt_values = value_all[:prompt_rows]
        start_state = (
            jnp.full((HEADS, row_count), very_low, jnp.float32),
            jnp.zeros((HEADS, row_count), jnp.float32),
            jnp.zeros((HEADS, row_count, HEAD_SIZE), jnp.float32),
        )

        def fold_prompt(state_in, key_piece, first_row):
            key_rows, value_rows = key_piece
            allowed = (
                query_pos[:, None]
                >= (first_row + jnp.arange(key_rows.shape[0], dtype=jnp.int32))[None, :]
            )
            return fold_scores(state_in, queries, key_rows, value_rows, allowed, score_scale)

        whole_keys, whole_values = (
            lax.all_gather(prompt_keys, ("context", "expert"), axis=0, tiled=True),
            lax.all_gather(prompt_values, ("context", "expert"), axis=0, tiled=True),
        )

        def scan_prompt(state_in, block_id):
            first_row = block_id * block_rows
            key_rows = lax.dynamic_slice_in_dim(whole_keys, first_row, block_rows, 0)
            value_rows = lax.dynamic_slice_in_dim(whole_values, first_row, block_rows, 0)
            return (fold_prompt(state_in, (key_rows, value_rows), first_row), None)

        state_out, unused_out = lax.scan(
            scan_prompt, start_state, jnp.arange(prompt_total // block_rows, dtype=jnp.int32)
        )
        state_out = fold_scores(
            state_out,
            queries,
            key_all[prompt_rows:],
            value_all[prompt_rows:],
            self_allowed,
            score_scale,
        )
        row_max, row_sum, weighted = state_out
        log_norm = row_max + jnp.log(row_sum)
        attn_heads = weighted / row_sum[..., None]
        attn_float = jnp.transpose(attn_heads, (1, 0, 2)).reshape(row_count, model_width)
        attended = attn_float.astype(jnp.bfloat16)
        residual = x_rows + jnp.dot(attended, w_out, preferred_element_type=jnp.float32)
        normed_two = rms_scale(residual, gain_two).astype(jnp.bfloat16)
        two_float = normed_two.astype(jnp.float32)
        routed_use = active * (route_ids < EXPERTS).astype(jnp.int32)
        expert_hot = (route_ids[..., None] == jnp.arange(EXPERTS, dtype=jnp.int32)).astype(
            jnp.int32
        ) * routed_use[..., None]
        flat_hot = expert_hot.reshape(row_count * TOP, EXPERTS)
        route_rank = jnp.sum((jnp.cumsum(flat_hot, axis=0) - 1) * flat_hot, axis=-1).reshape(
            row_count, TOP
        )
        slot_of = jnp.where(routed_use > 0, route_ids * capacity + route_rank, -1)
        select = (slot_range[:, None, None] == slot_of[None]).astype(jnp.bfloat16)
        send_rows = jnp.dot(
            jnp.sum(select, axis=-1), normed_two, preferred_element_type=jnp.float32
        ).astype(jnp.bfloat16)
        send_rows = send_rows.reshape(expert_group, local_experts, capacity, model_width)
        received = lax.all_to_all(send_rows, "expert", split_axis=0, concat_axis=0, tiled=True)
        gate_pre = jnp.einsum(
            "sepd,edf->sepf", received, w_gate, preferred_element_type=jnp.float32
        )
        up_pre = jnp.einsum("sepd,edf->sepf", received, w_up, preferred_element_type=jnp.float32)
        hidden = (jax.nn.silu(gate_pre) * up_pre).astype(jnp.bfloat16)
        expert_rows = jnp.einsum(
            "sepf,efd->sepd", hidden, w_down, preferred_element_type=jnp.float32
        ).astype(jnp.bfloat16)
        returned = lax.all_to_all(
            expert_rows, "expert", split_axis=0, concat_axis=0, tiled=True
        ).reshape(EXPERTS * capacity, model_width)
        route_out = jnp.stack(
            [
                jnp.dot(select[:, :, top_index].T, returned, preferred_element_type=jnp.float32)
                for top_index in range(TOP)
            ],
            axis=1,
        )

        def local_mix(two_in, router_in, prior_in, const_win, const_vin, route_in):
            return mixture(
                two_in, router_in, prior_in, const_win, const_vin, route_in, route_ids, active
            )

        mix_out, mix_back = jax.vjp(
            local_mix, two_float, router_f, prior_row, const_wf, const_vf, route_out
        )
        outputs_list.append((residual + mix_out).astype(jnp.bfloat16))
        upstream = out_grad[micro, 0, 0].astype(jnp.float32)
        two_grad, router_grad, prior_grad, const_wgrad, const_vgrad, route_grad = mix_back(upstream)
        slot_grad = jnp.zeros((EXPERTS * capacity, model_width), jnp.float32)
        for top_index in range(TOP):
            slot_grad = slot_grad + jnp.dot(
                select[:, :, top_index].astype(jnp.float32),
                route_grad[:, top_index],
                precision=highest,
            )
        slot_grad = slot_grad.astype(jnp.bfloat16).reshape(
            expert_group, local_experts, capacity, model_width
        )
        grad_in = lax.all_to_all(slot_grad, "expert", split_axis=0, concat_axis=0, tiled=True)
        gate_pre = jnp.einsum(
            "sepd,edf->sepf", received, w_gate, preferred_element_type=jnp.float32
        )
        up_pre = jnp.einsum("sepd,edf->sepf", received, w_up, preferred_element_type=jnp.float32)
        gate_act = jax.nn.silu(gate_pre)
        hidden = (gate_act * up_pre).astype(jnp.bfloat16)
        hidden_grad = jnp.einsum(
            "sepd,efd->sepf", grad_in, w_down, preferred_element_type=jnp.float32
        )
        sigma = jax.nn.sigmoid(gate_pre)
        gate_grad = (hidden_grad * up_pre * (sigma + gate_pre * sigma * (1.0 - sigma))).astype(
            jnp.bfloat16
        )
        up_grad = (hidden_grad * gate_act).astype(jnp.bfloat16)
        row_back = (
            jnp.einsum("sepf,edf->sepd", gate_grad, w_gate, preferred_element_type=jnp.float32)
            + jnp.einsum("sepf,edf->sepd", up_grad, w_up, preferred_element_type=jnp.float32)
        ).astype(jnp.bfloat16)
        expert_acc = (
            expert_acc[0]
            + jnp.einsum("sepd,sepf->edf", received, gate_grad, preferred_element_type=jnp.float32),
            expert_acc[1]
            + jnp.einsum("sepd,sepf->edf", received, up_grad, preferred_element_type=jnp.float32),
            expert_acc[2]
            + jnp.einsum("sepf,sepd->efd", hidden, grad_in, preferred_element_type=jnp.float32),
        )
        back_rows = lax.all_to_all(
            row_back, "expert", split_axis=0, concat_axis=0, tiled=True
        ).reshape(EXPERTS * capacity, model_width)
        ffn_grad = jnp.zeros((row_count, model_width), jnp.float32)
        for top_index in range(TOP):
            ffn_grad = ffn_grad + jnp.dot(
                select[:, :, top_index].T, back_rows, preferred_element_type=jnp.float32
            )
        two_total = two_grad + ffn_grad
        unused_two, norm_back = jax.vjp(rms_scale, residual, gain_two)
        resid_grad, gain_two_grad = norm_back(two_total)
        resid_total = upstream + resid_grad
        branch_grad = resid_total.astype(jnp.bfloat16)
        out_wgrad = jnp.dot(attended.T, branch_grad, preferred_element_type=jnp.float32)
        attn_grad = jnp.dot(branch_grad, w_out.T, preferred_element_type=jnp.float32).astype(
            jnp.bfloat16
        )
        attn_grad_h = attn_grad.reshape(row_count, HEADS, HEAD_SIZE)
        delta = jnp.sum(
            attn_grad_h.astype(jnp.float32) * attn_float.reshape(row_count, HEADS, HEAD_SIZE),
            axis=-1,
        ).T
        back_keys, back_values = (whole_keys, whole_values)

        def scan_back(query_acc, block_id):
            first_row = block_id * block_rows
            key_rows = lax.dynamic_slice_in_dim(back_keys, first_row, block_rows, 0)
            value_rows = lax.dynamic_slice_in_dim(back_values, first_row, block_rows, 0)
            allowed = (
                query_pos[:, None] >= (first_row + jnp.arange(block_rows, dtype=jnp.int32))[None, :]
            )
            query_part, key_part, value_part = score_grads(
                queries, key_rows, value_rows, allowed, log_norm, attn_grad_h, delta, score_scale
            )
            return (query_acc + query_part, (key_part, value_part))

        query_acc, (key_parts, value_parts) = lax.scan(
            scan_back,
            jnp.zeros((row_count, HEADS, HEAD_SIZE), jnp.float32),
            jnp.arange(prompt_total // block_rows, dtype=jnp.int32),
        )
        key_sum, value_sum = (
            lax.psum_scatter(
                key_parts.reshape(prompt_total, model_width).astype(jnp.bfloat16),
                ("context", "expert"),
                scatter_dimension=0,
                tiled=True,
            ).astype(jnp.float32),
            lax.psum_scatter(
                value_parts.reshape(prompt_total, model_width).astype(jnp.bfloat16),
                ("context", "expert"),
                scatter_dimension=0,
                tiled=True,
            ).astype(jnp.float32),
        )
        query_self, key_self, value_self = score_grads(
            queries,
            key_all[prompt_rows:],
            value_all[prompt_rows:],
            self_allowed,
            log_norm,
            attn_grad_h,
            delta,
            score_scale,
        )
        query_grad = (query_acc + query_self).reshape(row_count, model_width).astype(jnp.bfloat16)
        key_grad = jnp.concatenate([key_sum, key_self.reshape(CLEN, model_width)], axis=0).astype(
            jnp.bfloat16
        )
        value_grad = jnp.concatenate(
            [value_sum, value_self.reshape(CLEN, model_width)], axis=0
        ).astype(jnp.bfloat16)
        query_wgrad = jnp.dot(normed.T, query_grad, preferred_element_type=jnp.float32)
        key_wgrad = jnp.dot(normed.T, key_grad, preferred_element_type=jnp.float32)
        value_wgrad = jnp.dot(normed.T, value_grad, preferred_element_type=jnp.float32)
        normed_grad = (
            jnp.dot(query_grad, w_query.T, preferred_element_type=jnp.float32)
            + jnp.dot(key_grad, w_key.T, preferred_element_type=jnp.float32)
            + jnp.dot(value_grad, w_value.T, preferred_element_type=jnp.float32)
        )
        unused_one, norm_back_one = jax.vjp(rms_scale, x_rows, gain_one)
        input_grad, gain_one_grad = norm_back_one(normed_grad)
        token_grads.append((resid_total + input_grad).astype(jnp.bfloat16))
        prior_grads.append(prior_grad)
        dense_acc = jax.tree.map(
            add_pair,
            dense_acc,
            (
                gain_one_grad,
                query_wgrad,
                key_wgrad,
                value_wgrad,
                out_wgrad,
                gain_two_grad,
                router_grad,
                const_wgrad,
                const_vgrad,
            ),
        )
    dense_sum = lax.psum(dense_acc, ("dp", "context", "expert"))
    expert_sum = (
        lax.psum(expert_acc[0].astype(jnp.bfloat16), ("dp", "context")).astype(jnp.float32),
        lax.psum(expert_acc[1].astype(jnp.bfloat16), ("dp", "context")).astype(jnp.float32),
        lax.psum(expert_acc[2].astype(jnp.bfloat16), ("dp", "context")).astype(jnp.float32),
    )
    layer_out = jnp.stack(outputs_list)[:, None, None]
    input_out = jnp.stack(token_grads)[:, None, None]
    prior_out = jnp.stack(prior_grads)[:, None, None]
    return (
        layer_out,
        input_out,
        prior_out,
        dense_sum[0],
        dense_sum[1],
        dense_sum[2],
        dense_sum[3],
        dense_sum[4],
        dense_sum[5],
        dense_sum[6],
        dense_sum[7],
        dense_sum[8],
        expert_sum[0],
        expert_sum[1],
        expert_sum[2],
    )


def solution(mesh):
    return jax.shard_map(
        on_device,
        mesh=mesh,
        in_specs=(
            P(None, "dp", ("context", "expert"), None, None),
            P(None, "dp", ("context", "expert"), None, None),
            P(None, "dp", ("context", "expert"), None, None),
            P(None, "dp", ("context", "expert"), None, None),
            P(None, "dp", ("context", "expert")),
            P(),
            P(),
            P(),
            P(),
            P(),
            P(),
            P(),
            P(),
            P(),
            P("expert", None, None),
            P("expert", None, None),
            P("expert", None, None),
            P(None, "dp", ("context", "expert"), None, None),
        ),
        out_specs=(
            P(None, "dp", ("context", "expert"), None, None),
            P(None, "dp", ("context", "expert"), None, None),
            P(None, "dp", ("context", "expert"), None, None),
            P(),
            P(),
            P(),
            P(),
            P(),
            P(),
            P(),
            P(),
            P(),
            P("expert", None, None),
            P("expert", None, None),
            P("expert", None, None),
        ),
        check_vma=False,
    )
```

profile of v0, /device:TPU:1, one launch (start us, length us, event | category | flops | bytes accessed | tf_op | source)
XLA Modules:
  0.0 1209.2 jit_solution(41823571360074110)
XLA Ops:
  80.1 6.7 copy.161
  86.7 30.4 %all-gather.7.cloned.1.call-done = bf16[2048,12,64]{2,0,1:T(8,128)(2,1)} async-done(((bf16[64,12,64]{2,0,1:T(8,128)(2,1)}), bf16[2048,12,64]{2,0,1:T(8,128)(2,1)}) %all-gather.7.cloned.1.call-update) | async-done | bytes 3145744 | tf_op jit(solution)/shard_map/all_gather | solution.py:200
  117.2 6.7 copy.162
  124.4 64.9 %while.60 = (s32[]{:T(128)}, f32[12,192]{1,0:T(8,128)}, f32[12,192]{1,0:T(8,128)}, f32[12,192,64]{1,2,0:T(8,128)}, s32[4]{0:T(128)}, /*index=5*/bf16[2048,12,64]...) while((s32[]{:T(128)}, f32[12,192]{1,0:T(8,128)}, ...), condition=%wide.region_4.5_spmd.clone, body=%wide.region_1.4_spmd.clone.sunk | while | flops 317878592 | bytes 37324644 | solution.py:209
  127.0 4.9 fusion.583
  159.3 4.9 fusion.583
  190.7 6.7 copy.177
  206.3 11.8 all-gather.11.cloned.1.call-done
  218.1 6.7 copy.178
  225.4 63.4 %while.61 = (s32[]{:T(128)}, f32[12,192]{1,0:T(8,128)S(1)}, f32[12,192]{1,0:T(8,128)}, f32[12,192,64]{1,2,0:T(8,128)}, s32[4]{0:T(128)}, /*index=5*/bf16[2048,12...) while((s32[]{:T(128)}, f32[12,192]{1,0:T(8,128)S(1)}, ...), condition=%wide.region_27.28_spmd.clone, body=%wide.region_24.27_spmd.clone.sunk | while | flops 317878592 | bytes 37287752 | solution.py:209
  228.5 4.8 fusion.590
  244.1 4.8 fusion.590
  259.9 4.8 fusion.590
  275.7 4.8 fusion.590
  307.9 4.9 all-to-all-start
  353.7 4.9 fusion.122
  362.9 4.9 all-to-all-start.4
  367.8 5.0 fusion.125
  377.1 5.1 all-to-all-start.6
  382.2 6.1 multiply_convert_fusion.3
  391.4 4.9 all-to-all-start.1
  424.6 5.1 all-to-all-start.7
  447.0 5.3 all-to-all-done.5
  468.4 57.9 %while.63 = (s32[]{:T(128)}, f32[192,12,64]{0,2,1:T(8,128)S(1)}, bf16[4,512,12,64]{1,3,2,0:T(8,128)(2,1)}, bf16[4,512,12,64]{1,3,2,0:T(8,128)(2,1)}, s32[4]{0:T(...) while((s32[]{:T(128)}, f32[192,12,64]{0,2,1:T(8,128)S(1)}, ...), condition=%wide.region_80.81_spmd.clone, body=%wide.region_79.80_spmd.clone.sunk | while | flops 767706176 | bytes 95666400 | solution.py:346
  552.5 61.4 %while.62 = (s32[]{:T(128)}, f32[192,12,64]{0,2,1:T(8,128)}, bf16[4,512,12,64]{1,3,2,0:T(8,128)(2,1)}, bf16[4,512,12,64]{1,3,2,0:T(8,128)(2,1)}, s32[4]{0:T(128)...) while((s32[]{:T(128)}, f32[192,12,64]{0,2,1:T(8,128)}, ...), condition=%wide.region_61.62_spmd.clone, body=%wide.region_60.61_spmd.clone.sunk | while | flops 767706176 | bytes 95002528 | solution.py:346
  678.5 17.5 %reduce-scatter.19.cloned.1.call-done = bf16[64,768]{1,0:T(8,128)(2,1)} async-done(((bf16[2048,768]{1,0:T(8,128)(2,1)}), bf16[64,768]{1,0:T(8,128)(2,1)}) %reduce-scatter.19.cloned.1.call-update) | async-done | bytes 98320
  697.1 82.9 %reduce-scatter.13.cloned.1.call-done = bf16[64,768]{1,0:T(8,128)(2,1)} async-done(((bf16[2048,768]{1,0:T(8,128)(2,1)}), bf16[64,768]{1,0:T(8,128)(2,1)}) %reduce-scatter.13.cloned.1.call-update) | async-done | bytes 98320
  781.1 83.4 %reduce-scatter.15.cloned.1.call-done = bf16[64,768]{1,0:T(8,128)(2,1)} async-done(((bf16[2048,768]{1,0:T(8,128)(2,1)}), bf16[64,768]{1,0:T(8,128)(2,1)}) %reduce-scatter.15.cloned.1.call-update) | async-done | bytes 98320
  888.8 69.0 %all-reduce.16 = (f32[768]{0:T(1024)}, f32[768]{0:T(1024)}, f32[768,12]{0,1:T(8,128)}, f32[2,768,2]{1,2,0:T(2,128)}, f32[2,768]{1,0:T(2,128)}) all-reduce(f32[768]{0:T(1024)S(1)} %add.481, f32[768]{0:T(1024)S(1)} %copy-done.215, ...), channel_id=1, replica_groups=mesh['dp'=4,'context'=4,'expert'=8] {'dp','context','expert'}, use_global_device_ids=true, to_apply=%region_86.87 | all-reduce | flops 15360 | bytes 122880 | tf_op jit(solution)/shard_map/psum | solution.py:409
  960.2 61.0 %all-reduce.24.cloned.1.call-done = (bf16[1,768,2048]{2,1,0:T(8,128)(2,1)}, bf16[1,768,2048]{2,1,0:T(8,128)(2,1)}, bf16[1,2048,768]{2,1,0:T(8,128)(2,1)}) async-done(((bf16[1,768,2048]{2,1,0:T(8,128)(2,1)}, bf16[1,768,2048]{2,1,0:T(8,128)(2,1)}, bf16[1,2048,768]{2,1,0:T(8,128)(2,1)}), (bf16[1,768,2048]{2,1,0:T(8,128)(2,1)}, bf16[1,768,2048]{2,1,0:T(8,128)(2,1)}, ...) | async-done | bytes 9437200 | tf_op jit(solution)/shard_map/psum | solution.py:411
  1021.2 5.6 convert_element_type.475
  1033.5 158.8 %all-reduce.22.cloned.1.call-done = (f32[768,768]{1,0:T(8,128)}, f32[768,768]{1,0:T(8,128)}, f32[768,768]{1,0:T(8,128)}, f32[768,768]{1,0:T(8,128)}) async-done(((f32[768,768]{1,0:T(8,128)}, f32[768,768]{1,0:T(8,128)}, f32[768,768]{1,0:T(8,128)}, f32[768,768]{1,0:T(8,128)}), (f32[768,768]{1,0:T(8,128)}, f32[768,768]{1,0:T(8,128)}, f32[768,768]{1,0:T(8,128)}, ...) | async-done | bytes 9437200 | tf_op jit(solution)/shard_map/psum | solution.py:409
  (1200 shorter events, 554.9 us)
Async XLA Ops:
  7.2 375.0 %copy-start = (bf16[1,2048,768]{2,1,0:T(8,128)(2,1)S(1)}, bf16[1,2048,768]{2,1,0:T(8,128)(2,1)}, u32[]{:S(2)}) copy-start(bf16[1,2048,768]{2,1,0:T(8,128)(2,1)} %param.42) | copy-start | bytes 9437188
  7.2 72.9 %all-gather.5.cloned.1.call-start = ((), (), s32[]{:S(2)}) async-start(), calls=%async_computation.12 | async-start | bytes 6488064 | tf_op jit(solution)/shard_map/all_gather | solution.py:199
  8.1 32.0 %copy-start.126 = (f32[768]{0:T(1024)}, f32[768]{0:T(1024)S(1)}, u32[]{:S(2)}) copy-start(f32[768]{0:T(1024)S(1)} %convert_element_type.380) | copy-start | bytes 9220
  9.4 28.1 %copy-start.171 = (f32[192]{0:T(256)}, f32[192]{0:T(256)S(1)}, u32[]{:S(2)}) copy-start(f32[192]{0:T(256)S(1)} %fusion.374) | copy-start | bytes 2308
  12.9 104.3 %all-gather.7.cloned.1.call-start = ((), (), s32[]{:S(2)}) async-start(), calls=%async_computation.13 | async-start | bytes 6488064 | tf_op jit(solution)/shard_map/all_gather | solution.py:200
  16.5 174.2 %all-gather.9.cloned.1.call-start = ((), (), s32[]{:S(2)}) async-start(), calls=%async_computation.14 | async-start | bytes 6488064 | tf_op jit(solution)/shard_map/all_gather | solution.py:199
  16.5 23.6 %copy-start.174 = (f32[192]{0:T(256)}, f32[192]{0:T(256)S(1)}, u32[]{:S(2)}) copy-start(f32[192]{0:T(256)S(1)} %fusion.376) | copy-start | bytes 2308
  20.0 198.1 %all-gather.11.cloned.1.call-start = ((), (), s32[]{:S(2)}) async-start(), calls=%async_computation.15 | async-start | bytes 6488064 | tf_op jit(solution)/shard_map/all_gather | solution.py:200
  206.3 19.1 %copy-start.10 = (bf16[192,768]{0,1:T(8,128)(2,1)S(1)}, bf16[192,768]{0,1:T(8,128)(2,1)}, u32[]{:S(2)}) copy-start(bf16[192,768]{0,1:T(8,128)(2,1)} %copy.175) | copy-start | bytes 884740
  307.9 41.0 %all-to-all-start = ((bf16[8,1,36,768]{3,2,1,0:T(8,128)(2,1)}), bf16[8,1,36,768]{3,2,1,0:T(8,128)(2,1)}, u32[]{:S(2)}, u32[]{:S(2)}) async-start(bf16[8,1,36,768]{3,2,1,0:T(8,128)(2,1)} %bitcast.864), calls=%async_computation | async-start | bytes 983040 | tf_op jit(solution)/shard_map/all_to_all | solution.py:242
  348.9 14.1 %all-to-all-start.2 = ((bf16[8,1,36,768]{3,2,1,0:T(8,128)(2,1)}), bf16[8,1,36,768]{3,2,1,0:T(8,128)(2,1)}, u32[]{:S(2)}, u32[]{:S(2)}) async-start(bf16[8,1,36,768]{3,2,1,0:T(8,128)(2,1)} %bitcast.867), calls=%async_computation.2 | async-start | bytes 983040 | tf_op jit(solution)/shard_map/all_to_all | solution.py:242
  362.9 14.1 %all-to-all-start.4 = ((bf16[8,1,36,768]{3,2,1,0:T(8,128)(2,1)}), bf16[8,1,36,768]{3,2,1,0:T(8,128)(2,1)}, u32[]{:S(2)}, u32[]{:S(2)}) async-start(bf16[8,1,36,768]{3,2,1,0:T(8,128)(2,1)} %bitcast.865), calls=%async_computation.4 | async-start | bytes 983040 | tf_op jit(solution)/shard_map/all_to_all | solution.py:283
  377.1 14.3 %all-to-all-start.6 = ((bf16[8,1,36,768]{3,2,1,0:T(8,128)(2,1)}), bf16[8,1,36,768]{3,2,1,0:T(8,128)(2,1)}, u32[]{:S(2)}, u32[]{:S(2)}) async-start(bf16[8,1,36,768]{3,2,1,0:T(8,128)(2,1)} %bitcast.866), calls=%async_computation.6 | async-start | bytes 983040 | tf_op jit(solution)/shard_map/all_to_all | solution.py:283
  391.4 19.2 %all-to-all-start.1 = ((bf16[8,1,36,768]{3,2,1,0:T(8,128)(2,1)}), bf16[8,1,36,768]{3,2,1,0:T(8,128)(2,1)}, u32[]{:S(2)}, u32[]{:S(2)}) async-start(bf16[8,1,36,768]{3,2,1,0:T(8,128)(2,1)} %fusion.198), calls=%async_computation.1 | async-start | bytes 983040 | tf_op jit(solution)/shard_map/all_to_all | solution.py:251
  410.5 14.1 %all-to-all-start.3 = ((bf16[8,1,36,768]{3,2,1,0:T(8,128)(2,1)}), bf16[8,1,36,768]{3,2,1,0:T(8,128)(2,1)}, u32[]{:S(2)}, u32[]{:S(2)}) async-start(bf16[8,1,36,768]{3,2,1,0:T(8,128)(2,1)} %fusion.195), calls=%async_computation.3 | async-start | bytes 983040 | tf_op jit(solution)/shard_map/all_to_all | solution.py:251
  424.6 14.3 %all-to-all-start.7 = ((bf16[8,1,36,768]{3,2,1,0:T(8,128)(2,1)}), bf16[8,1,36,768]{3,2,1,0:T(8,128)(2,1)}, u32[]{:S(2)}, u32[]{:S(2)}) async-start(bf16[8,1,36,768]{3,2,1,0:T(8,128)(2,1)} %fusion.206), calls=%async_computation.7 | async-start | bytes 983040 | tf_op jit(solution)/shard_map/all_to_all | solution.py:310
  434.2 18.2 %copy-start.128 = (f32[192,12]{0,1:T(8,128)}, f32[192,12]{0,1:T(8,128)S(1)}, u32[]{:S(2)}) copy-start(f32[192,12]{0,1:T(8,128)S(1)} %add_multiply_fusion) | copy-start | bytes 27652
  434.4 18.1 %copy-start.130 = (f32[192,12]{0,1:T(8,128)}, f32[192,12]{0,1:T(8,128)S(1)}, u32[]{:S(2)}) copy-start(f32[192,12]{0,1:T(8,128)S(1)} %add_multiply_fusion.1) | copy-start | bytes 27652
  439.0 13.4 %all-to-all-start.5 = ((bf16[8,1,36,768]{3,2,1,0:T(8,128)(2,1)}), bf16[8,1,36,768]{3,2,1,0:T(8,128)(2,1)S(1)}, u32[]{:S(2)}, u32[]{:S(2)}) async-start(bf16[8,1,36,768]{3,2,1,0:T(8,128)(2,1)} %fusion.201), calls=%async_computation.5 | async-start | bytes 983040 | tf_op jit(solution)/shard_map/all_to_all | solution.py:310
  443.3 234.1 %reduce-scatter.17.cloned.1.call-start = ((), (), s32[]{:S(2)}) async-start(), calls=%async_computation.18 | async-start | bytes 3244032
  534.7 161.3 %reduce-scatter.19.cloned.1.call-start = ((), (), s32[]{:S(2)}) async-start(), calls=%async_computation.19 | async-start | bytes 3244032
  547.3 232.7 %reduce-scatter.13.cloned.1.call-start = ((), (), s32[]{:S(2)}) async-start(), calls=%async_computation.16 | async-start | bytes 3244032
  625.6 238.9 %reduce-scatter.15.cloned.1.call-start = ((), (), s32[]{:S(2)}) async-start(), calls=%async_computation.17 | async-start | bytes 3244032
  637.6 383.6 %all-reduce.24.cloned.1.call-start = ((), (), s32[]{:S(2)}) async-start(), calls=%async_computation.21 | async-start | bytes 18874368 | tf_op jit(solution)/shard_map/psum | solution.py:411
  661.6 530.7 %all-reduce.22.cloned.1.call-start = ((), (), s32[]{:S(2)}) async-start(), calls=%async_computation.20 | async-start | bytes 18874368 | tf_op jit(solution)/shard_map/psum | solution.py:409
  675.5 190.0 %copy-start.78 = (bf16[12,64,128]{2,1,0:T(8,128)(2,1)S(1)}, bf16[12,64,128]{2,1,0:T(8,128)(2,1)}, u32[]{:S(2)}) copy-start(bf16[12,64,128]{2,1,0:T(8,128)(2,1)} %fusion.211) | copy-start | bytes 589828
  677.4 188.9 %copy-start.135 = (bf16[12,64,128]{2,1,0:T(8,128)(2,1)S(1)}, bf16[12,64,128]{2,1,0:T(8,128)(2,1)}, u32[]{:S(2)}) copy-start(bf16[12,64,128]{2,1,0:T(8,128)(2,1)} %convolution_convert_fusion.11) | copy-start | bytes 589828
  678.5 188.5 %copy-start.74 = (bf16[64,768]{0,1:T(8,128)(2,1)}, bf16[64,768]{0,1:T(8,128)(2,1)S(1)}, u32[]{:S(2)}) copy-start(bf16[64,768]{0,1:T(8,128)(2,1)S(1)} %copy.212) | copy-start | bytes 294916
  697.1 172.1 %copy-start.76 = (bf16[64,768]{0,1:T(8,128)(2,1)}, bf16[64,768]{0,1:T(8,128)(2,1)S(1)}, u32[]{:S(2)}) copy-start(bf16[64,768]{0,1:T(8,128)(2,1)S(1)} %copy.214) | copy-start | bytes 294916
  781.0 86.0 %copy-start.81 = (bf16[64,768]{0,1:T(8,128)(2,1)}, bf16[64,768]{0,1:T(8,128)(2,1)S(1)}, u32[]{:S(2)}) copy-start(bf16[64,768]{0,1:T(8,128)(2,1)S(1)} %copy.208) | copy-start | bytes 294916
  887.0 70.8 %copy-start.252 = (f32[192]{0:T(256)S(1)}, f32[192]{0:T(256)}, u32[]{:S(2)}) copy-start(f32[192]{0:T(256)} %copy-done.251) | copy-start | bytes 2308
  887.0 70.8 %copy-start.250 = (f32[192]{0:T(256)S(1)}, f32[192]{0:T(256)}, u32[]{:S(2)}) copy-start(f32[192]{0:T(256)} %copy-done.249) | copy-start | bytes 2308
  (352 other events, 1313.4 us)
Sparse Core Ops, SparseCore 0:
  13.0 53.0 all-gather.4
  69.0 48.1 all-gather.6
  119.5 48.1 all-gather.8
  169.9 48.1 all-gather.10
  534.9 77.4 reduce-scatter.16
  616.2 79.7 reduce-scatter.18
  700.2 79.7 reduce-scatter.12
  784.6 79.7 reduce-scatter.14
  869.1 152.0 all-reduce.23
  1027.9 164.3 all-reduce.21
where the time goes:
time: 1220 us; the launch traced here: 1210 us
  waiting for transfers between devices  458 us (38%)
  matrix products  301 us (25%)
  local copies, waits for them, and re-layouts  196 us (16%)
  other arithmetic  114 us (9%)
  blocking collectives  69 us (6%)
  starting transfers between devices  39.6 us (3%)
  between operations  19 us (2%)
  loops' own time  12.8 us (1%)
    unnamed x14, waiting for transfers between devices  184 us
    psum x1, waiting for transfers between devices, on_device(): dense_sum = lax.psum(dense_acc, ('dp', 'context', 'expert'))  159 us
    unnamed x537, local copies, waits for them, and re-layouts  81.8 us
    psum x1, blocking collectives, on_device(): dense_sum = lax.psum(dense_acc, ('dp', 'context', 'expert'))  69 us
    psum x1, waiting for transfers between devices, on_device(): lax.psum(expert_acc[0].astype(jnp.bfloat16), ('dp', 'context'))  61 us
    dot_general x10, matrix products, fold_scores(): jnp.einsum('qhd,khd->hqk', queries, key_rows, preferred_element_type=jnp....  46 us
    all_gather x2, waiting for transfers between devices, on_device(): lax.all_gather(prompt_values, ('context', 'expert'), axis=0, tiled=True)  42.2 us
    dot_general x10, matrix products, fold_scores(): jnp.einsum('hqk,khd->hqd', weights.astype(jnp.bfloat16), value_rows, pref...  34.4 us
  transfers between devices with their start and end apart: 18, of which 13 were waited for; matrix products, arithmetic and copies ran while one was open for 34% of the time, Pallas kernels for 0%

commit v1 on v0

v1 whole, which is shorter than its diff:
```python
import functools
import math

import jax
import jax.numpy as jnp
from jax import lax
from jax.experimental import pallas as pl
from jax.experimental.pallas import tpu as pltpu
from jax.sharding import Mesh, PartitionSpec as P

HEADS = 12
HEAD_SIZE = 64
EXPERTS = 8
CONSTS = 2
TARGETS = 12
CLEN = 128
QUAD = 4
LANES = 128

norm_eps = 1e-05
very_low = -1e30
highest = lax.Precision.HIGHEST
f32 = jnp.float32
bf16 = jnp.bfloat16
CHIPS = ("context", "z")
ALL_CHIPS = ("dp", "context", "z")
EXPERT = ("z", "core")


def dot_nn(left, right, **kw):
    return jnp.dot(left, right, preferred_element_type=f32, **kw)


def dot_nt(left, right, **kw):
    return lax.dot_general(left, right, (((1,), (1,)), ((), ())), preferred_element_type=f32, **kw)


def dot_tn(left, right, **kw):
    return lax.dot_general(left, right, (((0,), (0,)), ((), ())), preferred_element_type=f32, **kw)


def iota(shape, dim):
    return lax.broadcasted_iota(jnp.int32, shape, dim)


def params():
    return pltpu.CompilerParams(vmem_limit_bytes=63_400_000)


def head_masks(dtype):
    lane_head = iota((1, QUAD * HEAD_SIZE), 1) // HEAD_SIZE
    return [(lane_head == h).astype(f32).astype(dtype) for h in range(QUAD)]


def spread(rows, prompt, dtype):
    masks = head_masks(dtype)
    return jnp.concatenate(
        [rows[:prompt] * m for m in masks] + [rows[prompt:] * m for m in masks], axis=0
    )


def gather_heads(stacked, prompt, dtype):
    masks = head_masks(dtype)
    top, low = 0.0, 0.0
    first = QUAD * prompt
    for h in range(QUAD):
        top = top + stacked[h * prompt : (h + 1) * prompt] * masks[h]
        low = low + stacked[first + h * CLEN : first + (h + 1) * CLEN] * masks[h]
    return jnp.concatenate([top, low], axis=0)


def key_slots(core, keys, prompt, shape, dim):
    j = iota(shape, dim)
    half = keys // 2
    other = (j >= half).astype(jnp.int32)
    slot = ((j - other * half) // prompt) * 2 + jnp.where(other > 0, 1 - core, core)
    return slot * prompt + (j & (prompt - 1))


def attn_fwd_kernel(
    base_ref, normed_ref, near_ref, far_ref, wq_ref, wkv_ref, o_ref, lse_ref, q_ref, kv_ref
):
    prompt = q_ref.shape[0] - CLEN
    keys = kv_ref.shape[0] - CLEN
    half = keys // 2
    wide = QUAD * HEAD_SIZE
    masks = head_masks(bf16)
    masks_f = head_masks(f32)
    ones = jnp.ones((8, LANES), f32)

    def to_row(column):
        spare = jnp.where(iota((column.shape[0], LANES), 1) == 0, column, 0.0)
        return dot_nt(ones, spare, precision=highest)

    q = dot_nn(normed_ref[...], wq_ref[...]).astype(bf16).astype(f32)
    q_ref[...] = (q * (1.0 / math.sqrt(HEAD_SIZE))).astype(bf16)
    w_kv = wkv_ref[...]
    for rows, at in ((near_ref, 0), (far_ref, half)):
        for r in range(0, half, 512):
            kv_ref[at + r : at + r + 512] = dot_nn(rows[r : r + 512], w_kv).astype(bf16)
    kv_ref[keys:] = dot_nn(normed_ref[prompt:], w_kv).astype(bf16)
    q_top, q_low = q_ref[:prompt], q_ref[prompt:]
    q_p = jnp.concatenate([q_top * m for m in masks], axis=0)
    s = dot_nt(q_p, kv_ref[:keys, :wide])
    limit = base_ref[0] + (iota((QUAD * prompt, 1), 0) & (prompt - 1))
    s = jnp.where(key_slots(base_ref[1], keys, prompt, (1, keys), 1) <= limit, s, very_low)
    top = jnp.max(s, axis=1, keepdims=True)
    p = jnp.exp(s - top)
    total = jnp.sum(p, axis=1, keepdims=True)
    out = dot_nn(p.astype(bf16), kv_ref[:keys, wide:]) * (1.0 / total)
    lse_ref[:, : QUAD * prompt] = to_row(top + jnp.log(total))
    o_ref[:prompt] = sum(out[h * prompt : (h + 1) * prompt] * masks_f[h] for h in range(QUAD))
    low_out = 0.0
    per = 2
    for part in range(QUAD // per):
        hs = range(part * per, (part + 1) * per)
        rows = per * CLEN
        q_c = jnp.concatenate([q_low * masks[h] for h in hs], axis=0)
        s = dot_nt(q_c, kv_ref[:keys, :wide])
        own = dot_nt(q_c, kv_ref[keys:, :wide])
        own = jnp.where(
            iota((1, CLEN), 1) <= (iota((rows, 1), 0) & (CLEN - 1)), own, very_low
        )
        top = jnp.maximum(
            jnp.max(s, axis=1, keepdims=True), jnp.max(own, axis=1, keepdims=True)
        )
        p = jnp.exp(s - top)
        p_own = jnp.exp(own - top)
        total = jnp.sum(p, axis=1, keepdims=True) + jnp.sum(p_own, axis=1, keepdims=True)
        out = dot_nn(p.astype(bf16), kv_ref[:keys, wide:])
        out = out + dot_nn(p_own.astype(bf16), kv_ref[keys:, wide:])
        out = out * (1.0 / total)
        at = QUAD * prompt + part * rows
        lse_ref[:, at : at + rows] = to_row(top + jnp.log(total))
        for i, h in enumerate(hs):
            low_out = low_out + out[i * CLEN : (i + 1) * CLEN] * masks_f[h]
    o_ref[prompt:] = low_out


def attn_fwd(base, normed, near, far, w_query, w_kv):
    rows, width = normed.shape
    half = near.shape[0]
    every = 2 * half + CLEN
    quads = HEADS // QUAD
    wide = QUAD * HEAD_SIZE
    col = lambda n, w=wide: pl.BlockSpec((n, w), lambda g, b: (0, g))
    whole = lambda n: pl.BlockSpec((n, width), lambda g, b: (0, 0))
    return pl.pallas_call(
        attn_fwd_kernel,
        grid_spec=pltpu.PrefetchScalarGridSpec(
            num_scalar_prefetch=1,
            grid=(quads,),
            in_specs=[whole(rows), whole(half), whole(half), col(width), col(width, 2 * wide)],
            out_specs=[
                col(rows),
                pl.BlockSpec((None, 8, QUAD * rows), lambda g, b: (g, 0, 0)),
                col(rows),
                col(every, 2 * wide),
            ],
        ),
        out_shape=[
            jax.ShapeDtypeStruct((rows, width), f32),
            jax.ShapeDtypeStruct((quads, 8, QUAD * rows), f32),
            jax.ShapeDtypeStruct((rows, width), bf16),
            jax.ShapeDtypeStruct((every, 2 * width), bf16),
        ],
        compiler_params=params(),
        cost_estimate=pl.CostEstimate(
            flops=16 * rows * every * width + 4 * every * width * width,
            bytes_accessed=4 * every * width,
            transcendentals=rows * every * HEADS,
        ),
        name="attn_fwd",
    )(base, normed, near, far, w_query, w_kv)


def attn_bwd_kernel(
    base_ref, q_ref, kv_ref, do_ref, o_ref, lse_ref, dq_ref, dkv_ref, qm, dom, dqt, *, block
):
    prompt = q_ref.shape[0] - CLEN
    keys = kv_ref.shape[0] - CLEN
    wide = QUAD * HEAD_SIZE
    qm[...] = spread(q_ref[...], prompt, bf16)
    dom[...] = spread(do_ref[...], prompt, bf16)
    prod = spread(do_ref[...].astype(f32) * o_ref[...], prompt, f32)
    delta = dot_nt(jnp.ones((8, prod.shape[1]), f32), prod, precision=highest)[0:1]
    lse = lse_ref[0:1, :]
    first = QUAD * prompt
    limit = base_ref[0] + (iota((1, first), 1) & (prompt - 1))
    q_all, do_all = qm[...], dom[...]

    def one(rows, mask):
        kk, vv = kv_ref[rows, :wide], kv_ref[rows, wide:]
        p = jnp.exp(dot_nt(kk, q_all) - lse)
        p = mask(p)
        ds = p * (dot_nt(vv, do_all) - delta)
        pb, dsb = p.astype(bf16), ds.astype(bf16)
        dkv_ref[rows, :wide] = dot_nn(dsb, q_all).astype(bf16)
        dkv_ref[rows, wide:] = dot_nn(pb, do_all).astype(bf16)
        return dot_tn(kk, dsb)

    def own_mask(p):
        lane = iota((1, p.shape[1]), 1)
        own_row = jnp.where(lane < first, -1, (lane - first) & (CLEN - 1))
        return jnp.where(iota((CLEN, 1), 0) <= own_row, p, 0.0)

    dqt[...] = one(pl.ds(keys, CLEN), own_mask)

    def step(i, unused):
        at = pl.multiple_of(i * block, block)

        def mask(p):
            half = (at >= keys // 2).astype(jnp.int32)
            core = jnp.where(half > 0, 1 - base_ref[1], base_ref[1])
            j = at - half * (keys // 2) + iota((block, 1), 0)
            where = ((j // prompt) * 2 + core) * prompt + (j & (prompt - 1))
            seen = where <= limit
            return jnp.concatenate([jnp.where(seen, p[:, :first], 0.0), p[:, first:]], axis=1)

        dqt[...] += one(pl.ds(at, block), mask)
        return unused

    lax.fori_loop(0, keys // block, step, 0)
    dq = gather_heads(dqt[...].T, prompt, f32)
    dq_ref[...] = (dq * (1.0 / math.sqrt(HEAD_SIZE))).astype(bf16)


def attn_bwd(base, q, kv, do, o, lse, block=256):
    rows, width = q.shape
    every = kv.shape[0]
    quads = HEADS // QUAD
    wide = QUAD * HEAD_SIZE
    col = lambda n, w=wide: pl.BlockSpec((n, w), lambda g, b: (0, g))
    return pl.pallas_call(
        functools.partial(attn_bwd_kernel, block=block),
        grid_spec=pltpu.PrefetchScalarGridSpec(
            num_scalar_prefetch=1,
            grid=(quads,),
            in_specs=[
                col(rows), col(every, 2 * wide), col(rows), col(rows),
                pl.BlockSpec((None, 8, QUAD * rows), lambda g, b: (g, 0, 0)),
            ],
            out_specs=[col(rows), col(every, 2 * wide)],
            scratch_shapes=[
                pltpu.VMEM((QUAD * rows, wide), bf16),
                pltpu.VMEM((QUAD * rows, wide), bf16),
                pltpu.VMEM((wide, QUAD * rows), f32),
            ],
        ),
        out_shape=[
            jax.ShapeDtypeStruct((rows, width), bf16),
            jax.ShapeDtypeStruct((every, 2 * width), bf16),
        ],
        compiler_params=params(),
        cost_estimate=pl.CostEstimate(
            flops=40 * rows * every * width,
            bytes_accessed=8 * every * width,
            transcendentals=rows * every * HEADS,
        ),
        name="attn_bwd",
    )(base, q, kv, do, o, lse)


def route_kernel(
    x_ref, attn_ref, wout_ref, gain_ref, wr_ref, prior_ref, eff_ref, efft_ref, og_ref,
    resid_ref, two_ref, ch_ref, send_ref, sel_ref, selt_ref, gate_ref, *, cap,
):
    rows, width = x_ref.shape
    slots = EXPERTS * cap
    resid = x_ref[...].astype(f32) + dot_nn(attn_ref[...].astype(bf16), wout_ref[...])
    resid_ref[...] = resid
    inv = lax.rsqrt(jnp.mean(resid * resid, axis=1, keepdims=True) + norm_eps)
    two = (resid * inv * gain_ref[...]).astype(bf16)
    two_ref[...] = two
    lane = iota((1, LANES), 1)
    logits = dot_nn(two, wr_ref[...]) + prior_ref[...]
    masked = jnp.where(lane < TARGETS, logits, very_low)
    e = jnp.exp(masked - jnp.max(masked, axis=1, keepdims=True))
    ch = e * (1.0 / jnp.sum(e, axis=1, keepdims=True))
    for j in range(CONSTS):
        at = TARGETS + 2 * j
        diff = logits[:, at + 1 : at + 2] - logits[:, at : at + 1]
        ch = jnp.where(lane == at, 1.0 / (1.0 + jnp.exp(diff)), ch)
        ch = jnp.where(lane == at + 1, 1.0 / (1.0 + jnp.exp(-diff)), ch)
    ch_ref[...] = ch
    target = iota((16, rows), 0)
    hot_t = ((target == efft_ref[0:1, :]) | (target == efft_ref[1:2, :])).astype(f32)
    before = (iota((rows, rows), 0) < iota((rows, rows), 1)).astype(f32).astype(bf16)
    rank_t = dot_nn(hot_t.astype(bf16), before)
    rank_t = jnp.where(hot_t > 0.0, rank_t, -1.0)
    place = iota((cap, 1), 0).astype(f32)
    sel = jnp.concatenate(
        [(place == rank_t[i : i + 1, :]).astype(f32) for i in range(EXPERTS)], axis=0
    )
    sel_b = sel.astype(bf16)
    sel_ref[...] = sel_b
    hot = ((lane == eff_ref[:, 0:1]) | (lane == eff_ref[:, 1:2])).astype(f32)
    after = (iota((rows, rows), 0) > iota((rows, rows), 1)).astype(f32).astype(bf16)
    rank = dot_nn(after, hot.astype(bf16))
    rank = jnp.where(hot > 0.0, rank, -1.0)
    slot = iota((1, slots), 1)
    widen = (slot // cap == iota((LANES, 1), 0)).astype(f32).astype(bf16)
    rank_s = dot_nn(rank.astype(bf16), widen)
    selt_ref[...] = (rank_s == (slot % cap).astype(f32)).astype(f32).astype(bf16)
    ch_s = dot_nn(sel, ch, precision=highest)
    of_slot = iota((slots, 1), 0) // cap
    gate = jnp.sum(jnp.where(lane == of_slot, ch_s, 0.0), axis=1, keepdims=True)
    gate_ref[...] = jnp.broadcast_to(gate, gate_ref.shape)
    send_ref[:, :width] = dot_nn(sel_b, two).astype(bf16)
    send_ref[:, width:] = (gate * dot_nn(sel_b, og_ref[...])).astype(bf16)


def route(x, attn, w_out, gain, wr, prior, eff, efft, og, cap):
    rows, width = x.shape
    slots = EXPERTS * cap
    return pl.pallas_call(
        functools.partial(route_kernel, cap=cap),
        out_shape=[
            jax.ShapeDtypeStruct((rows, width), f32),
            jax.ShapeDtypeStruct((rows, width), bf16),
            jax.ShapeDtypeStruct((rows, LANES), f32),
            jax.ShapeDtypeStruct((slots, 2 * width), bf16),
            jax.ShapeDtypeStruct((slots, rows), bf16),
            jax.ShapeDtypeStruct((rows, slots), bf16),
            jax.ShapeDtypeStruct((slots, LANES), f32),
        ],
        compiler_params=params(),
        cost_estimate=pl.CostEstimate(
            flops=6 * rows * width * width, bytes_accessed=4 * width * width, transcendentals=0
        ),
        name="route",
    )(x, attn, w_out, gain, wr, prior, eff, efft, og)


def expert_kernel(
    x_ref, g_ref, wg_ref, wu_ref, wd_ref, out_ref, hid_ref, gg_ref, ug_ref, fwd, back
):
    step = pl.program_id(0)
    width = x_ref.shape[1]

    @pl.when(step == 0)
    def _():
        fwd[...] = jnp.zeros_like(fwd)
        back[...] = jnp.zeros_like(back)

    x, g = x_ref[...], g_ref[...]
    gate = dot_nn(x, wg_ref[...])
    up = dot_nn(x, wu_ref[...])
    hid_grad = dot_nt(g, wd_ref[...])
    sig = 1.0 / (1.0 + jnp.exp(-gate))
    act = gate * sig
    hid = (act * up).astype(bf16)
    gg = (hid_grad * up * (sig + act * (1.0 - sig))).astype(bf16)
    ug = (hid_grad * act).astype(bf16)
    hid_ref[...] = hid
    gg_ref[...] = gg
    ug_ref[...] = ug
    fwd[...] += dot_nn(hid, wd_ref[...])
    back[...] += dot_nt(gg, wg_ref[...]) + dot_nt(ug, wu_ref[...])

    @pl.when(step == pl.num_programs(0) - 1)
    def _():
        out_ref[:, :width] = fwd[...].astype(bf16)
        out_ref[:, width:] = back[...].astype(bf16)


def experts(rows_in, w_gate, w_up, w_down, tile=256):
    rows = rows_in.shape[0]
    width = rows_in.shape[1] // 2
    hidden = w_gate.shape[2]
    half = lambda i: pl.BlockSpec((rows, width), lambda t, i=i: (0, i))
    inner = pl.BlockSpec((None, width, tile), lambda t: (0, 0, t))
    mid = pl.BlockSpec((rows, tile), lambda t: (0, t))
    return pl.pallas_call(
        expert_kernel,
        grid=(hidden // tile,),
        in_specs=[half(0), half(1), inner, inner, pl.BlockSpec((None, tile, width), lambda t: (0, t, 0))],
        out_specs=[pl.BlockSpec((rows, 2 * width), lambda t: (0, 0)), mid, mid, mid],
        out_shape=[jax.ShapeDtypeStruct((rows, 2 * width), bf16)]
        + [jax.ShapeDtypeStruct((rows, hidden), bf16)] * 3,
        scratch_shapes=[pltpu.VMEM((rows, width), f32), pltpu.VMEM((rows, width), f32)],
        compiler_params=params(),
        cost_estimate=pl.CostEstimate(
            flops=14 * rows * width * hidden,
            bytes_accessed=6 * width * hidden,
            transcendentals=rows * hidden,
        ),
        name="experts",
    )(rows_in, rows_in, w_gate, w_up, w_down)


def expert_wgrad_kernel(*refs, count):
    ins, (dg_ref, du_ref, dd_ref, xt) = refs[: 5 * count], refs[5 * count :]
    rows = ins[0].shape[0]

    @pl.when(pl.program_id(0) == 0)
    def _():
        for m in range(count):
            xt[:, m * rows : (m + 1) * rows] = ins[5 * m][...].T

    g, hid, gg, ug = (
        jnp.concatenate([ins[5 * m + i][...] for m in range(count)], axis=0) for i in range(1, 5)
    )
    dg_ref[...] = dot_nn(xt[...], gg).astype(bf16)
    du_ref[...] = dot_nn(xt[...], ug).astype(bf16)
    dd_ref[...] = dot_tn(hid, g).astype(bf16)


def expert_wgrad(parts, tile=256):
    rows = parts[0][0].shape[0]
    width = parts[0][0].shape[1] // 2
    hidden = parts[0][1].shape[1]
    half = lambda i: pl.BlockSpec((rows, width), lambda t, i=i: (0, i))
    mid = pl.BlockSpec((rows, tile), lambda t: (0, t))
    specs, args = [], []
    for rows_in, hid, gg, ug in parts:
        specs += [half(0), half(1), mid, mid, mid]
        args += [rows_in, rows_in, hid, gg, ug]
    inner = pl.BlockSpec((width, tile), lambda t: (0, t))
    return pl.pallas_call(
        functools.partial(expert_wgrad_kernel, count=len(parts)),
        grid=(hidden // tile,),
        in_specs=specs,
        out_specs=[inner, inner, pl.BlockSpec((tile, width), lambda t: (t, 0))],
        out_shape=[
            jax.ShapeDtypeStruct((width, hidden), bf16),
            jax.ShapeDtypeStruct((width, hidden), bf16),
            jax.ShapeDtypeStruct((hidden, width), bf16),
        ],
        scratch_shapes=[pltpu.VMEM((width, len(parts) * rows), bf16)],
        compiler_params=params(),
        cost_estimate=pl.CostEstimate(
            flops=6 * len(parts) * rows * width * hidden,
            bytes_accessed=6 * width * hidden,
            transcendentals=0,
        ),
        name="expert_wgrad",
    )(*args)


def combine_kernel(
    resid_ref, two_ref, ch_ref, eff_ref, og_ref, ret_ref, sel_ref, selt_ref, gate_ref,
    wout_ref, gain_ref, wr_ref, cv_ref,
    mixed_ref, rtot_ref, branch_ref, ag_ref, dl_ref, small_ref, *, cap,
):
    rows, width = resid_ref.shape
    slots = EXPERTS * cap
    lane = iota((1, LANES), 1)
    resid, two_b, ch = resid_ref[...], two_ref[...], ch_ref[...]
    two = two_b.astype(f32)
    og_b = og_ref[...]
    og = og_b.astype(f32)
    eo = ret_ref[:, :width].astype(f32)
    sel, selt = sel_ref[...], selt_ref[...]
    hot = ((lane == eff_ref[:, 0:1]) | (lane == eff_ref[:, 1:2])).astype(f32)
    dgate = jnp.sum(dot_nn(sel, og_b) * eo, axis=1, keepdims=True)
    by_target = jnp.where(lane == iota((slots, 1), 0) // cap, dgate, 0.0)
    dval = dot_nn(selt.astype(f32), by_target, precision=highest)
    self_dot = jnp.sum(og * two, axis=1, keepdims=True)
    cv_dot = dot_nt(og_b, cv_ref[...])
    gates = ch * hot
    keep = gates[:, EXPERTS + 1 : EXPERTS + 2]
    dval = jnp.where(lane == EXPERTS + 1, self_dot, dval)
    mixed = resid + dot_nn(selt, (gate_ref[:, 0:1] * eo).astype(bf16))
    dl_const = jnp.zeros((rows, LANES), f32)
    coef_cv = jnp.zeros((rows, LANES), f32)
    for j in range(CONSTS):
        e, at = EXPERTS + 2 + j, TARGETS + 2 * j
        a0, a1 = ch[:, at : at + 1], ch[:, at + 1 : at + 2]
        gate = gates[:, e : e + 1]
        with_cv = cv_dot[:, e : e + 1]
        dval = jnp.where(lane == e, a0 * self_dot + a1 * with_cv, dval)
        keep = keep + gate * a0
        mixed = mixed + (gate * a1) * cv_ref[e : e + 1, :].astype(f32)
        coef_cv = jnp.where(lane == TARGETS + 2 * CONSTS + j, gate * a1, coef_cv)
        da0, da1 = gate * self_dot, gate * with_cv
        mean = a0 * da0 + a1 * da1
        dl_const = jnp.where(lane == at, a0 * (da0 - mean), dl_const)
        dl_const = jnp.where(lane == at + 1, a1 * (da1 - mean), dl_const)
    mixed = mixed + keep * two
    mixed_ref[...] = mixed.astype(bf16)
    ch = jnp.where(lane < TARGETS, ch, 0.0)
    dch = hot * dval
    dl = ch * (dch - jnp.sum(ch * dch, axis=1, keepdims=True)) + dl_const
    dl_ref[...] = dl
    dl_hi = dl.astype(bf16)
    dl_lo = (dl - dl_hi.astype(f32)).astype(bf16)
    cc_hi = coef_cv.astype(bf16)
    cc_lo = (coef_cv - cc_hi.astype(f32)).astype(bf16)
    small = dot_tn(dl_hi, two_b) + dot_tn(dl_lo, two_b) + dot_tn(cc_hi, og_b) + dot_tn(cc_lo, og_b)
    two_grad = (
        keep * og
        + dot_nt(dl_hi, wr_ref[...])
        + dot_nt(dl_lo, wr_ref[...])
        + dot_nn(selt, ret_ref[:, width:])
    )
    inv = lax.rsqrt(jnp.mean(resid * resid, axis=1, keepdims=True) + norm_eps)
    xhat = resid * inv
    gain_grad = jnp.sum(two_grad * xhat, axis=0, keepdims=True)
    small_ref[...] = jnp.where(
        iota((small_ref.shape[0], 1), 0) == TARGETS + 3 * CONSTS, gain_grad, small[: small_ref.shape[0]]
    )
    scaled = two_grad * gain_ref[...]
    rtot = og + inv * (scaled - xhat * jnp.mean(scaled * xhat, axis=1, keepdims=True))
    rtot_ref[...] = rtot
    branch = rtot.astype(bf16)
    branch_ref[...] = branch
    ag_ref[...] = dot_nt(branch, wout_ref[...]).astype(bf16)


def combine(resid, two, ch, eff, og, ret, sel, selt, gate, w_out, gain, wr, cv, cap):
    rows, width = resid.shape
    return pl.pallas_call(
        functools.partial(combine_kernel, cap=cap),
        out_shape=[
            jax.ShapeDtypeStruct((rows, width), bf16),
            jax.ShapeDtypeStruct((rows, width), f32),
            jax.ShapeDtypeStruct((rows, width), bf16),
            jax.ShapeDtypeStruct((rows, width), bf16),
            jax.ShapeDtypeStruct((rows, LANES), f32),
            jax.ShapeDtypeStruct((24, width), f32),
        ],
        compiler_params=params(),
        cost_estimate=pl.CostEstimate(
            flops=6 * rows * width * width, bytes_accessed=4 * width * width, transcendentals=0
        ),
        name="combine",
    )(resid, two, ch, eff, og, ret, sel, selt, gate, w_out, gain, wr, cv)


def back_proj_kernel(
    dkv_ref, own_ref, wkv_ref, near_ref, far_ref, normed_ref, dq_ref, wq_ref,
    give_ref, keep_ref, mine_ref, gain_ref, *, steps,
):
    t = pl.program_id(0)

    @pl.when(t == 0)
    def _():
        prompt = normed_ref.shape[0] - CLEN
        mine = dot_nt(dq_ref[...], wq_ref[...])
        low = mine[prompt:] + dot_nt(own_ref[...], wkv_ref[...])
        mine_ref[:prompt] = mine[:prompt]
        mine_ref[prompt:] = low
        normed = normed_ref[...].astype(f32)
        total = jnp.sum(mine[:prompt] * normed[:prompt], axis=0, keepdims=True)
        total = total + jnp.sum(low * normed[prompt:], axis=0, keepdims=True)
        gain_ref[...] = jnp.broadcast_to(total, gain_ref.shape)

    part = dot_nt(dkv_ref[...], wkv_ref[...])

    @pl.when(t < steps)
    def _():
        give_ref[...] = part.astype(bf16)
        gain_ref[...] += jnp.sum(part * far_ref[...].astype(f32), axis=0, keepdims=True)

    @pl.when(t >= steps)
    def _():
        keep_ref[...] = part
        gain_ref[...] += jnp.sum(part * near_ref[...].astype(f32), axis=0, keepdims=True)


def back_proj(dkv, w_kv, near, far, normed, dq, w_query, block=256):
    rows, width = normed.shape
    half = near.shape[0]
    steps = half // block
    whole = lambda n, w=width: pl.BlockSpec((n, w), lambda t: (0, 0))
    first = pl.BlockSpec((block, width), lambda t: (jnp.minimum(t, steps - 1), 0))
    last = pl.BlockSpec((block, width), lambda t: (jnp.maximum(t - steps, 0), 0))
    return pl.pallas_call(
        functools.partial(back_proj_kernel, steps=steps),
        grid=(2 * steps,),
        in_specs=[
            pl.BlockSpec((block, 2 * width), lambda t: ((t + steps) % (2 * steps), 0)),
            pl.BlockSpec((CLEN, 2 * width), lambda t: (2 * half // CLEN, 0)),
            whole(width, 2 * width), last, first, whole(rows), whole(rows), whole(width),
        ],
        out_specs=[first, last, whole(rows), whole(8)],
        out_shape=[
            jax.ShapeDtypeStruct((half, width), bf16),
            jax.ShapeDtypeStruct((half, width), f32),
            jax.ShapeDtypeStruct((rows, width), f32),
            jax.ShapeDtypeStruct((8, width), f32),
        ],
        compiler_params=params(),
        cost_estimate=pl.CostEstimate(
            flops=8 * half * width * width, bytes_accessed=12 * half * width, transcendentals=0
        ),
        name="back_proj",
    )(dkv, dkv, w_kv, near, far, normed, dq, w_query)


PIECES = 8
UNIT = 48
PACK = 160


def dense_wgrad_kernel(core_ref, *refs, count):
    ins = refs[: 9 * count]
    gain_ref, give_ref, keep_ref, every_t, normed_t, attn_t = refs[9 * count :]
    t = pl.program_id(0)
    half_steps = PIECES // 2
    piece = (t + half_steps * (1 - core_ref[0])) % PIECES
    rows, width = ins[2].shape
    prompt = rows - CLEN
    half = ins[0].shape[0]
    each = 2 * half + CLEN

    @pl.when(t == 0)
    def _():
        for m in range(count):
            near, far, normed, attn = (ins[9 * m + i] for i in range(4))
            at = m * each
            every_t[:, at : at + half] = near[...].T
            every_t[:, at + half : at + 2 * half] = far[...].T
            every_t[:, at + 2 * half : at + each] = normed[prompt:].T
            normed_t[:, m * rows : (m + 1) * rows] = normed[...].T
            attn_t[:, m * rows : (m + 1) * rows] = attn[...].astype(bf16).T

    stack = lambda i: jnp.concatenate([ins[9 * m + i][...] for m in range(count)], axis=0)

    def write(grad):
        low = grad.astype(bf16)
        small = sum(ins[9 * m + 7][...] for m in range(count))
        gain = sum(ins[9 * m + 8][0:1, :] for m in range(count)) / gain_ref[...]
        small = jnp.where(
            iota((small.shape[0], 1), 0) == TARGETS + 3 * CONSTS + 1, gain, small
        ).astype(bf16)

        def into(out_ref):
            out_ref[:, 3 * UNIT :, :] = jnp.zeros((16, PACK - 3 * UNIT, LANES), bf16)
            for k in range(16):
                for j in range(3):
                    out_ref[k, j * UNIT : (j + 1) * UNIT, :] = low[
                        k * UNIT : (k + 1) * UNIT, j * LANES : (j + 1) * LANES
                    ]
            for i in range(width // LANES):

                @pl.when(piece == i)
                def _():
                    block = small[:, i * LANES : (i + 1) * LANES]
                    out_ref[0, 3 * UNIT : 3 * UNIT + 16, :] = block[:16]
                    out_ref[1, 3 * UNIT : 3 * UNIT + 8, :] = block[16:24]

        @pl.when(t < half_steps)
        def _():
            into(give_ref)

        @pl.when(t >= half_steps)
        def _():
            into(keep_ref)

    @pl.when(piece < 2)
    def _():
        write(dot_nn(normed_t[...], stack(4)))

    @pl.when((piece >= 2) & (piece < 6))
    def _():
        write(dot_nn(every_t[...], stack(5)))

    @pl.when(piece >= 6)
    def _():
        write(dot_nn(attn_t[...], stack(6)))


def dense_wgrad(core, gain, parts):
    near, _, normed = parts[0][:3]
    rows, width = normed.shape
    half = near.shape[0]
    each = 2 * half + CLEN
    steps = PIECES // 2
    cols = 4 * width // PIECES
    piece = lambda t, c: (t + steps * (1 - c[0])) % PIECES
    whole = lambda n: pl.BlockSpec((n, width), lambda t, c: (0, 0))
    part = lambda n, lo, hi: pl.BlockSpec(
        (n, cols), lambda t, c: (0, jnp.clip(piece(t, c) - lo, 0, hi))
    )
    specs, args = [], []
    for p in parts:
        specs += [
            whole(half), whole(half), whole(rows), whole(rows),
            part(rows, 0, 1), part(each, 2, 3), part(rows, 6, 1), whole(24), whole(8),
        ]
        args += list(p)
    out = lambda f: pl.BlockSpec((16, PACK, LANES), lambda t, c: (f(t), 0, 0))
    count = len(parts)
    return pl.pallas_call(
        functools.partial(dense_wgrad_kernel, count=count),
        grid_spec=pltpu.PrefetchScalarGridSpec(
            num_scalar_prefetch=1,
            grid=(PIECES,),
            in_specs=specs + [whole(1)],
            out_specs=[
                out(lambda t: jnp.minimum(t, steps - 1)), out(lambda t: jnp.maximum(t - steps, 0))
            ],
            scratch_shapes=[
                pltpu.VMEM((width, count * each), bf16),
                pltpu.VMEM((width, count * rows), bf16),
                pltpu.VMEM((width, count * rows), bf16),
            ],
        ),
        out_shape=[jax.ShapeDtypeStruct((16 * steps, PACK, LANES), bf16)] * 2,
        compiler_params=params(),
        cost_estimate=pl.CostEstimate(
            flops=4 * count * each * width * width,
            bytes_accessed=6 * count * each * width,
            transcendentals=0,
        ),
        name="dense_wgrad",
    )(core, *args, gain)


def unpack_kernel(core_ref, mine_ref, other_ref, *outs):
    first = core_ref[0] == 0
    steps = PIECES // 2
    width = outs[0].shape[0]
    sub = QUAD * HEAD_SIZE // LANES
    per = width // LANES
    small_ref = outs[4]

    def take(i, k, lo, hi):
        a = mine_ref[(i % steps) * 16 + k, lo:hi, :]
        b = other_ref[(i % steps) * 16 + k, lo:hi, :]
        pick = first if i < steps else jnp.logical_not(first)
        return jnp.where(pick, a.astype(f32), b.astype(f32))

    for i in range(PIECES):
        for j in range(3):
            block = i * 3 + j
            if block < per:
                out, at = outs[0], block
            elif block < 3 * per:
                g, r = divmod(block - per, 2 * sub)
                out, at = outs[1 + r // sub], g * sub + r % sub
            else:
                out, at = outs[3], block - 3 * per
            for k in range(16):
                out[k * UNIT : (k + 1) * UNIT, at * LANES : (at + 1) * LANES] = take(
                    i, k, j * UNIT, (j + 1) * UNIT
                )
        if i < per:
            cols = slice(i * LANES, (i + 1) * LANES)
            small_ref[:16, cols] = take(i, 0, 3 * UNIT, 3 * UNIT + 16)
            small_ref[16:, cols] = take(i, 1, 3 * UNIT, 3 * UNIT + 16)[:8]


def unpack(core, mine, other, width):
    vmem = pl.BlockSpec(memory_space=pltpu.VMEM)
    return pl.pallas_call(
        unpack_kernel,
        in_specs=[pl.BlockSpec(memory_space=pltpu.SMEM), vmem, vmem],
        out_specs=[vmem] * 5,
        out_shape=[jax.ShapeDtypeStruct((width, width), f32)] * 4
        + [jax.ShapeDtypeStruct((24, width), f32)],
        compiler_params=params(),
        cost_estimate=pl.CostEstimate(
            flops=4 * width * width, bytes_accessed=24 * width * width, transcendentals=0
        ),
        name="unpack",
    )(core, mine, other)


def swap_cores(rows):
    return lax.ppermute(rows, "core", [(0, 1), (1, 0)])


def exchange(blocks, axes):
    return lax.all_to_all(blocks, axes, split_axis=0, concat_axis=0, tiled=True)


def spread_out(piece, axes):
    count = lax.axis_size(axes)
    return exchange(jnp.broadcast_to(piece[None], (count,) + piece.shape), axes)


def after(value, *others):
    return lax.optimization_barrier((value, *others))[0]


def on_device(
    tokens, prior_logits, routes, drops, cont_lengths, norm_gain, w_query, w_key, w_value, w_out,
    ffn_gain, w_router, w_const, const_vec, w_gate, w_up, w_down, out_grad,
):
    micros, rows, width = tokens.shape[0], tokens.shape[3], tokens.shape[4]
    prompt = rows - CLEN
    cap = -(-(rows * 3 // 16) // 8) * 8
    quads, wide = HEADS // QUAD, QUAD * HEAD_SIZE
    chips = lax.axis_size(CHIPS)
    half = chips * prompt
    core = lax.axis_index("core").astype(jnp.int32)
    base = jnp.stack([(lax.axis_index(CHIPS).astype(jnp.int32) * 2 + core) * prompt, core])
    score_scale = 1.0 / math.sqrt(HEAD_SIZE)
    gain_one = norm_gain.astype(f32)
    gain_two = ffn_gain.astype(f32).reshape(1, width)

    x = tokens[:, 0, 0]
    x_f = x.astype(f32)
    inv_one = lax.rsqrt(jnp.mean(x_f * x_f, axis=-1, keepdims=True) + norm_eps)
    normed = (x_f * inv_one * gain_one).astype(bf16)
    gathered = [spread_out(normed[0, :prompt], CHIPS)]
    for m in range(1, micros):
        gathered.append(spread_out(normed[m, :prompt], CHIPS))

    wr = jnp.concatenate(
        [w_router] + [w_const[j] for j in range(CONSTS)]
        + [jnp.zeros((width, LANES - TARGETS - 2 * CONSTS), bf16)], axis=1,
    )
    cv = jnp.zeros((LANES, width), bf16).at[EXPERTS + 2 : EXPERTS + 2 + CONSTS].set(const_vec)
    w_kv = jnp.concatenate(
        [w[:, g * wide : (g + 1) * wide] for g in range(quads) for w in (w_key, w_value)], axis=1
    )
    row_ids = jnp.arange(rows, dtype=jnp.int32)
    og = out_grad[:, 0, 0]
    live = row_ids[None] < prompt + cont_lengths[:, 0]
    active = (1 - drops[:, 0, 0]) * live[..., None].astype(jnp.int32)
    eff = jnp.where(active > 0, routes[:, 0, 0], -1)
    efft = jnp.swapaxes(eff, 1, 2)
    prior = jnp.pad(prior_logits[:, 0, 0], ((0, 0), (0, 0), (0, LANES - TARGETS)))

    st = []
    for m in range(micros):
        s = {}
        s["normed"] = normed[m]
        if m:
            gathered[m] = after(gathered[m], st[m - 1]["attn"])
        s["near"] = gathered[m].reshape(half, width)
        s["far"] = swap_cores(s["near"])
        s["attn"], s["lse"], s["q"], s["kv"] = attn_fwd(
            base, s["normed"], s["near"], s["far"], w_query, w_kv
        )
        s["resid"], s["two"], s["ch"], send, s["sel"], s["selt"], s["gate"] = route(
            x[m], s["attn"], w_out, gain_two, wr, prior[m], eff[m], efft[m], og[m], cap
        )
        s["recv"] = exchange(send.reshape(EXPERTS, cap, 2 * width), EXPERT).reshape(
            EXPERTS * cap, 2 * width
        )
        st.append(s)
    for s in st:
        ret, s["hid"], s["gg"], s["ug"] = experts(s["recv"], w_gate, w_up, w_down)
        s["ret"] = exchange(ret.reshape(EXPERTS, cap, 2 * width), EXPERT).reshape(
            EXPERTS * cap, 2 * width
        )
    wide_grads = expert_wgrad([(s["recv"], s["hid"], s["gg"], s["ug"]) for s in st])
    st[0]["ret"] = after(st[0]["ret"], wide_grads)
    wide_sum = lax.psum(tuple(wide_grads), ("dp", "context"))

    mixed, prior_grads, parts = [], [], []
    for m, s in enumerate(st):
        out, s["rtot"], branch, ag, dl, small = combine(
            s["resid"], s["two"], s["ch"], eff[m], og[m], s["ret"], s["sel"], s["selt"], s["gate"],
            w_out, gain_two, wr, cv, cap,
        )
        mixed.append(out)
        prior_grads.append(dl[:, :TARGETS])
        dq, dkv = attn_bwd(base, s["q"], s["kv"], ag, s["attn"], s["lse"])
        give, keep, s["mine"], gain = back_proj(
            dkv, w_kv, s["near"], s["far"], s["normed"], dq, w_query
        )
        keep = (keep + swap_cores(give).astype(f32)).astype(bf16)
        s["scatter"] = exchange(keep.reshape(chips, prompt, width), CHIPS)
        parts.append(
            (s["near"], s["far"], s["normed"], s["attn"], dq, dkv, branch, small, gain)
        )
    core_arg = core.reshape(1)
    give, keep = dense_wgrad(core_arg, gain_one.reshape(1, width), parts)
    keep = (keep.astype(f32) + swap_cores(give).astype(f32)).astype(bf16)
    own = jnp.sum(exchange(keep, ALL_CHIPS).astype(f32), axis=0).astype(bf16)
    own = after(own, wide_sum)
    own = spread_out(own, ALL_CHIPS)
    *dense, rest = unpack(core_arg, own, swap_cores(own), width)
    token_grads = []
    for m, s in enumerate(st):
        total = jnp.sum(s["scatter"].astype(f32), axis=0)
        grad = (s["mine"] + jnp.pad(total, ((0, CLEN), (0, 0)))) * gain_one
        xhat = x_f[m] * inv_one[m]
        grad = inv_one[m] * (grad - xhat * jnp.mean(grad * xhat, axis=-1, keepdims=True))
        token_grads.append((s["rtot"] + grad).astype(bf16))
    lift = lambda parts: jnp.stack(parts)[:, None, None]
    return (
        lift(mixed),
        lift(token_grads),
        lift(prior_grads),
        rest[TARGETS + 3 * CONSTS + 1],
        *dense,
        rest[TARGETS + 3 * CONSTS],
        rest[:TARGETS].T,
        jnp.stack([rest[TARGETS + 2 * j : TARGETS + 2 * j + 2].T for j in range(CONSTS)]),
        rest[TARGETS + 2 * CONSTS : TARGETS + 3 * CONSTS],
        *(g.astype(f32)[None] for g in wide_sum),
    )


def solution(mesh):
    shape = mesh.devices.shape
    split = Mesh(
        mesh.devices.reshape(shape[0], shape[1], shape[2] // 2, 2), ("dp", "context", "z", "core")
    )
    slot = P(None, "dp", ("context", "z", "core"), None, None)
    expert = P(("z", "core"), None, None)
    return jax.shard_map(
        on_device,
        mesh=split,
        in_specs=(
            slot, slot, slot, slot, P(None, "dp", ("context", "z", "core")),
            *(P(),) * 9,
            *(expert,) * 3,
            slot,
        ),
        out_specs=(slot, slot, slot, *(P(),) * 9, *(expert,) * 3),
        check_vma=False,
    )
```

time: 1220 us -> 515 us (0.42)
  waiting for transfers between devices: 458 us -> 116 us
  matrix products: 301 us -> 0 us
  Pallas kernels: 0 us -> 225 us
  local copies, waits for them, and re-layouts: 196 us -> 32.2 us
  other arithmetic: 114 us -> 38.6 us
  blocking collectives: 69 us -> 0 us
  starting transfers between devices: 39.6 us -> 78.1 us
  loops' own time: 12.8 us -> 0 us
    dot_general x142 -> x0, matrix products: 301 us -> none  [the longest x10 46 us: fold_scores(): jnp.einsum('qhd,khd->hqk', queries, key_rows, preferred_element_type=jnp....]
    pallas_call x0 -> x15, Pallas kernels: none -> 225 us  [the longest x2 54 us: attn_bwd(): pl.pallas_call(functools.partial(attn_bwd_kernel, block=block), grid_spec...]
    psum x2 -> x1, waiting for transfers between devices: 220 us -> 0.02 us  [on_device(): wide_sum = lax.psum(tuple(wide_grads), ('dp', 'context'))]
    unnamed x14 -> x1, waiting for transfers between devices: 184 us -> 0.54 us
    all_to_all x8 -> x10, waiting for transfers between devices: 11.8 us -> 112 us  [exchange(): return lax.all_to_all(blocks, axes, split_axis=0, concat_axis=0, tiled=True)]
    psum x1 -> x0, blocking collectives: 69 us -> none  [on_device(): dense_sum = lax.psum(dense_acc, ('dp', 'context', 'expert'))]
    unnamed x537 -> x74, local copies, waits for them, and re-layouts: 81.8 us -> 13.8 us
    reduce_sum x36 -> x5, other arithmetic: 49.2 us -> 5.25 us  [the longest x2 3.28 us: on_device(): total = jnp.sum(s['scatter'].astype(f32), axis=0)]
  transfers between devices with their start and end apart: 18 -> 17, of which waited for: 13 -> 7; matrix products, arithmetic and copies ran while one was open for 34% -> 11% of each run, Pallas kernels for 0% -> 43%
where the time goes in v1:
time: 515 us; the launch traced here: 505 us
  Pallas kernels  225 us (44%)
  waiting for transfers between devices  116 us (23%)
  starting transfers between devices  78.1 us (15%)
  other arithmetic  38.6 us (7%)
  local copies, waits for them, and re-layouts  32.2 us (6%)
  between operations  15 us (3%)
    all_to_all x10, waiting for transfers between devices, exchange(): return lax.all_to_all(blocks, axes, split_axis=0, concat_axis=0, tiled=True)  112 us
    all_to_all x10, starting transfers between devices, exchange(): return lax.all_to_all(blocks, axes, split_axis=0, concat_axis=0, tiled=True)  65.4 us
    pallas_call x2, Pallas kernels, attn_bwd(): pl.pallas_call(functools.partial(attn_bwd_kernel, block=block), grid_spec...  54 us
    pallas_call x2, Pallas kernels, attn_fwd(): pl.pallas_call(attn_fwd_kernel, grid_spec=pltpu.PrefetchScalarGridSpec(nu...  44.4 us
    pallas_call x2, Pallas kernels, back_proj(): pl.pallas_call(functools.partial(back_proj_kernel, steps=steps), grid=(2...  29.7 us
    pallas_call x1, Pallas kernels, dense_wgrad(): pl.pallas_call(functools.partial(dense_wgrad_kernel, count=count), grid_s...  27.1 us
    pallas_call x2, Pallas kernels, experts(): pl.pallas_call(expert_kernel, grid=(hidden // tile,), in_specs=[half(0),...  25.1 us
    pallas_call x2, Pallas kernels, combine(): pl.pallas_call(functools.partial(combine_kernel, cap=cap), out_shape=[jax...  14.5 us
  transfers between devices with their start and end apart: 17, of which 7 were waited for; matrix products, arithmetic and copies ran while one was open for 11% of the time, Pallas kernels for 43%

profile of v1, /device:TPU:1, one launch (start us, length us, event | category | flops | bytes accessed | tf_op | source)
XLA Modules:
  0.0 504.7 jit_solution(15271738088627131710)
XLA Ops:
  11.8 8.6 %all-to-all-start = ((bf16[16,64,768]{2,1,0:T(8,128)(2,1)}), bf16[16,64,768]{2,1,0:T(8,128)(2,1)}, u32[]{:S(2)}, u32[]{:S(2)}) async-start(bf16[16,64,768]{2,1,0:T(8,128)(2,1)} %broadcast_in_dim.66), calls=%async_computation | async-start | bytes 3145728 | tf_op jit(solution)/shard_map/all_to_all | solution.py:767
  22.0 19.1 %all-to-all-done = bf16[16,64,768]{2,1,0:T(8,128)(2,1)} async-done(((bf16[16,64,768]{2,1,0:T(8,128)(2,1)}), bf16[16,64,768]{2,1,0:T(8,128)(2,1)}, u32[]{:S(2)}, u32[]{:S(2)}) %all-to-all-start) | async-done | bytes 1572896 | tf_op jit(solution)/shard_map/all_to_all | solution.py:767
  42.4 5.4 %all-to-all-start.3 = ((bf16[16,64,768]{2,1,0:T(8,128)(2,1)}), bf16[16,64,768]{2,1,0:T(8,128)(2,1)}, u32[]{:S(2)}, u32[]{:S(2)}) async-start(bf16[16,64,768]{2,1,0:T(8,128)(2,1)} %broadcast_in_dim.70), calls=%async_computation.3 | async-start | bytes 3145728 | tf_op jit(solution)/shard_map/all_to_all | solution.py:767
  62.7 22.3 %attn_fwd.2 = (f32[192,768]{1,0:T(8,128)}, f32[3,8,768]{2,1,0:T(8,128)}, bf16[192,768]{1,0:T(8,128)(2,1)}, bf16[2176,1536]{1,0:T(8,128)(2,1)}) custom-call(s32[2]{0:T(128)} %pad_add_fusion.base_ref, bf16[192,768]{1,0:T(8,128)(2,1)} %get-tuple-element.206.normed_ref.refs_2_, bf16[1024,768]{1,0:T(8,128)(2,1)} %bitcast.7.near_ref.refs_0_, ...), custom_call_target="tpu_custom_call" | custom-call | flops 10267656192 | bytes 6684672 | tf_op jit(solution)/shard_map/attn_fwd/pallas_call | solution.py:148
  91.1 5.1 %route.2 = (f32[192,768]{1,0:T(8,128)}, bf16[192,768]{1,0:T(8,128)(2,1)}, f32[192,128]{1,0:T(8,128)}, bf16[320,1536]{1,0:T(8,128)(2,1)}, bf16[320,192]{1,0:T(8,1...) custom-call(bf16[192,768]{1,0:T(8,128)(2,1)} %get-tuple-element.224.x_ref, ...), custom_call_target="tpu_custom_call" | custom-call | flops 679477248 | bytes 2359296 | tf_op jit(solution)/shard_map/route/pallas_call | solution.py:316
  96.2 5.5 %all-to-all-start.1 = ((bf16[8,40,1536]{2,1,0:T(8,128)(2,1)}), bf16[8,40,1536]{2,1,0:T(8,128)(2,1)S(1)}, u32[]{:S(2)}, u32[]{:S(2)}) async-start(bf16[8,40,1536]{2,1,0:T(8,128)(2,1)} %bitcast.142), calls=%async_computation.1 | async-start | bytes 1966080 | tf_op jit(solution)/shard_map/all_to_all | solution.py:767
  102.9 22.1 %attn_fwd.3 = (f32[192,768]{1,0:T(8,128)}, f32[3,8,768]{2,1,0:T(8,128)}, bf16[192,768]{1,0:T(8,128)(2,1)}, bf16[2176,1536]{1,0:T(8,128)(2,1)}) custom-call(s32[2]{0:T(128)} %pad_add_fusion.base_ref, bf16[192,768]{1,0:T(8,128)(2,1)} %get-tuple-element.207.normed_ref.refs_11_, bf16[1024,768]{1,0:T(8,128)(2,1)} %bitcast.26.near_ref.refs_9_, ...), custom_call_target="tpu_custom_call" | custom-call | flops 10267656192 | bytes 6684672 | tf_op jit(solution)/shard_map/attn_fwd/pallas_call | solution.py:148
  125.0 5.1 %route.3 = (f32[192,768]{1,0:T(8,128)}, bf16[192,768]{1,0:T(8,128)(2,1)}, f32[192,128]{1,0:T(8,128)}, bf16[320,1536]{1,0:T(8,128)(2,1)}, bf16[320,192]{1,0:T(8,1...) custom-call(bf16[192,768]{1,0:T(8,128)(2,1)} %get-tuple-element.223.x_ref, ...), custom_call_target="tpu_custom_call" | custom-call | flops 679477248 | bytes 2359296 | tf_op jit(solution)/shard_map/route/pallas_call | solution.py:316
  130.2 4.8 all-to-all-start.4
  136.2 12.6 %experts.2 = (bf16[320,1536]{1,0:T(8,128)(2,1)}, bf16[320,2048]{1,0:T(8,128)(2,1)}, bf16[320,2048]{1,0:T(8,128)(2,1)}, bf16[320,2048]{1,0:T(8,128)(2,1)}) custom-call(bf16[320,1536]{1,0:T(8,128)(2,1)} %bitcast.138, bf16[320,1536]{1,0:T(8,128)(2,1)} %bitcast.139, bf16[1,768,2048]{2,1,0:T(8,128)(2,1)} %wg_ref.3, bf16[1,768,2048]{2,1,0:T(8,128)(2,1)} %wu_ref.3, ...), custom_call_target="tpu_custom_call" | custom-call | flops 7046430720 | bytes 9437184 | tf_op jit(solution)/shard_map/experts/pallas_call | solution.py:374
  149.4 4.3 all-to-all-start.2
  153.7 12.5 %experts.3 = (bf16[320,1536]{1,0:T(8,128)(2,1)}, bf16[320,2048]{1,0:T(8,128)(2,1)}, bf16[320,2048]{1,0:T(8,128)(2,1)}, bf16[320,2048]{1,0:T(8,128)(2,1)}) custom-call(bf16[320,1536]{1,0:T(8,128)(2,1)} %bitcast.143, bf16[320,1536]{1,0:T(8,128)(2,1)} %bitcast.144, bf16[1,768,2048]{2,1,0:T(8,128)(2,1)} %wg_ref.3, bf16[1,768,2048]{2,1,0:T(8,128)(2,1)} %wu_ref.3, ...), custom_call_target="tpu_custom_call" | custom-call | flops 7046430720 | bytes 9437184 | tf_op jit(solution)/shard_map/experts/pallas_call | solution.py:374
  166.3 13.1 %expert_wgrad.1 = (bf16[768,2048]{1,0:T(8,128)(2,1)}, bf16[768,2048]{1,0:T(8,128)(2,1)}, bf16[2048,768]{1,0:T(8,128)(2,1)}) custom-call(bf16[320,1536]{1,0:T(8,128)(2,1)} %bitcast.140, bf16[320,1536]{1,0:T(8,128)(2,1)} %bitcast.141, bf16[320,2048]{1,0:T(8,128)(2,1)} %get-tuple-element.100.refs_2_, bf16[320,2048]{1,0:T(8,128)(2,1)} %get-tuple-element.101.refs_3_, ...), custom_call_target="tpu_custom_call" | custom-call | flops 6039797760 | bytes 9437184 | tf_op jit(solution)/shard_map/expert_wgrad/pallas_call | solution.py:420
  179.4 4.8 all-to-all-start.5
  185.0 7.2 %combine.2 = (bf16[192,768]{1,0:T(8,128)(2,1)}, f32[192,768]{1,0:T(8,128)}, bf16[192,768]{1,0:T(8,128)(2,1)}, bf16[192,768]{1,0:T(8,128)(2,1)}, f32[192,128]{1,0:T(8,128)}, /*index=5*/f32[24,768]{1,0:T(8,128)}) custom-call(f32[192,768]{1,0:T(8,128)} %get-tuple-element.95.resid_ref, bf16[192,768]{1,0:T(8,128)(2,1)} %get-tuple-element.96.two_ref, ...), custom_call_target="tpu_custom_call" | custom-call | flops 679477248 | bytes 2359296 | tf_op jit(solution)/shard_map/combine/pallas_call | solution.py:513
  192.2 27.0 %attn_bwd.2 = (bf16[192,768]{1,0:T(8,128)(2,1)}, bf16[2176,1536]{1,0:T(8,128)(2,1)}) custom-call(s32[2]{0:T(128)} %pad_add_fusion.base_ref, bf16[192,768]{1,0:T(8,128)(2,1)} %get-tuple-element.126.q_ref, bf16[2176,1536]{1,0:T(8,128)(2,1)} %get-tuple-element.127.kv_ref, bf16[192,768]{1,0:T(8,128)(2,1)} %get-tuple-element.128.do_ref, ...), custom_call_target="tpu_custom_call" | custom-call | flops 12834570240 | bytes 13369344 | tf_op jit(solution)/shard_map/attn_bwd/pallas_call | solution.py:234
  219.2 15.1 %back_proj.2 = (bf16[1024,768]{1,0:T(8,128)(2,1)}, f32[1024,768]{1,0:T(8,128)}, f32[192,768]{1,0:T(8,128)}, f32[8,768]{1,0:T(8,128)}) custom-call(bf16[2176,1536]{1,0:T(8,128)(2,1)} %get-tuple-element.130.dkv_ref.own_ref.refs_5_, bf16[2176,1536]{1,0:T(8,128)(2,1)} %get-tuple-element.130.dkv_ref.own_ref.refs_5_, bf16[768,1536]{1,0:T(8,128)(2,1)} %copy-done, ...), custom_call_target="tpu_custom_call" | custom-call | flops 4831838208 | bytes 9437184 | tf_op jit(solution)/shard_map/back_proj/pallas_call | solution.py:569
  235.6 7.3 %combine.3 = (bf16[192,768]{1,0:T(8,128)(2,1)}, f32[192,768]{1,0:T(8,128)}, bf16[192,768]{1,0:T(8,128)(2,1)}, bf16[192,768]{1,0:T(8,128)(2,1)}, f32[192,128]{1,0:T(8,128)}, /*index=5*/f32[24,768]{1,0:T(8,128)}) custom-call(f32[192,768]{1,0:T(8,128)} %get-tuple-element.117.resid_ref, bf16[192,768]{1,0:T(8,128)(2,1)} %get-tuple-element.118.two_ref, ...), custom_call_target="tpu_custom_call" | custom-call | flops 679477248 | bytes 2359296 | tf_op jit(solution)/shard_map/combine/pallas_call | solution.py:513
  242.9 27.0 %attn_bwd.3 = (bf16[192,768]{1,0:T(8,128)(2,1)}, bf16[2176,1536]{1,0:T(8,128)(2,1)}) custom-call(s32[2]{0:T(128)} %pad_add_fusion.base_ref, bf16[192,768]{1,0:T(8,128)(2,1)} %get-tuple-element.136.q_ref, bf16[2176,1536]{1,0:T(8,128)(2,1)} %get-tuple-element.137.kv_ref, bf16[192,768]{1,0:T(8,128)(2,1)} %get-tuple-element.138.do_ref, ...), custom_call_target="tpu_custom_call" | custom-call | flops 12834570240 | bytes 13369344 | tf_op jit(solution)/shard_map/attn_bwd/pallas_call | solution.py:234
  269.9 14.7 %back_proj.3 = (bf16[1024,768]{1,0:T(8,128)(2,1)}, f32[1024,768]{1,0:T(8,128)}, f32[192,768]{1,0:T(8,128)}, f32[8,768]{1,0:T(8,128)}) custom-call(bf16[2176,1536]{1,0:T(8,128)(2,1)} %get-tuple-element.140.dkv_ref.own_ref.refs_14_, bf16[2176,1536]{1,0:T(8,128)(2,1)} %get-tuple-element.140.dkv_ref.own_ref.refs_14_, bf16[768,1536]{1,0:T(8,128)(2,1)} %copy-done, ...), custom_call_target="tpu_custom_call" | custom-call | flops 4831838208 | bytes 9437184 | tf_op jit(solution)/shard_map/back_proj/pallas_call | solution.py:569
  284.5 27.1 %dense_wgrad.1 = (bf16[64,160,128]{2,1,0:T(8,128)(2,1)}, bf16[64,160,128]{2,1,0:T(8,128)(2,1)}) custom-call(s32[1]{0:T(128)} %bitcast.2.core_ref, bf16[1024,768]{1,0:T(8,128)(2,1)} %bitcast.7.near_ref.refs_0_, bf16[1024,768]{1,0:T(8,128)(2,1)} %collective-permute-done.far_ref.refs_1_, bf16[192,768]{1,0:T(8,128)(2,1)} %get-tuple-element.206.normed_ref.refs_2_, ...), custom_call_target="tpu_custom_call" | custom-call | flops 10267656192 | bytes 20054016 | tf_op jit(solution)/shard_map/dense_wgrad/pallas_call | solution.py:686
  317.2 6.7 %all-to-all-start.6 = ((bf16[16,64,768]{2,1,0:T(8,128)(2,1)}), bf16[16,64,768]{2,1,0:T(8,128)(2,1)S(1)}, u32[]{:S(2)}, u32[]{:S(2)}) async-start(bf16[16,64,768]{2,1,0:T(8,128)(2,1)} %bitcast.134), calls=%async_computation.6 | async-start | bytes 3145728 | tf_op jit(solution)/shard_map/all_to_all | solution.py:767
  323.9 4.8 add_convert_fusion
  328.7 28.5 %all-to-all-done.6 = bf16[16,64,768]{2,1,0:T(8,128)(2,1)S(1)} async-done(((bf16[16,64,768]{2,1,0:T(8,128)(2,1)}), bf16[16,64,768]{2,1,0:T(8,128)(2,1)S(1)}, u32[]{:S(2)}, u32[]{:S(2)}) %all-to-all-start.6) | async-done | bytes 1572896 | tf_op jit(solution)/shard_map/all_to_all | solution.py:767
  358.3 10.0 %all-to-all-start.8 = ((bf16[64,160,128]{2,1,0:T(8,128)(2,1)}), bf16[64,160,128]{2,1,0:T(8,128)(2,1)S(1)}, u32[]{:S(2)}, u32[]{:S(2)}) async-start(bf16[64,160,128]{2,1,0:T(8,128)(2,1)} %add_convert_fusion), calls=%async_computation.8 | async-start | bytes 5242880 | tf_op jit(solution)/shard_map/all_to_all | solution.py:767
  376.5 24.0 %all-to-all-done.8 = bf16[64,160,128]{2,1,0:T(8,128)(2,1)S(1)} async-done(((bf16[64,160,128]{2,1,0:T(8,128)(2,1)}), bf16[64,160,128]{2,1,0:T(8,128)(2,1)S(1)}, u32[]{:S(2)}, u32[]{:S(2)}) %all-to-all-start.8) | async-done | bytes 2621472 | tf_op jit(solution)/shard_map/all_to_all | solution.py:767
  400.5 4.4 all-to-all-start.7
  405.4 18.7 %all-to-all-done.7 = bf16[16,64,768]{2,1,0:T(8,128)(2,1)} async-done(((bf16[16,64,768]{2,1,0:T(8,128)(2,1)}), bf16[16,64,768]{2,1,0:T(8,128)(2,1)}, u32[]{:S(2)}, u32[]{:S(2)}) %all-to-all-start.7) | async-done | bytes 1572896 | tf_op jit(solution)/shard_map/all_to_all | solution.py:767
  425.9 10.8 %all-to-all-start.9 = ((bf16[64,160,128]{2,1,0:T(8,128)(2,1)}), bf16[64,160,128]{2,1,0:T(8,128)(2,1)S(1)}, u32[]{:S(2)}, u32[]{:S(2)}) async-start(bf16[64,160,128]{2,1,0:T(8,128)(2,1)} %broadcast_in_dim.75), calls=%async_computation.9 | async-start | bytes 5242880 | tf_op jit(solution)/shard_map/all_to_all | solution.py:767
  446.0 21.4 %all-to-all-done.9.mine_ref = bf16[64,160,128]{2,1,0:T(8,128)(2,1)S(1)} async-done(((bf16[64,160,128]{2,1,0:T(8,128)(2,1)}), bf16[64,160,128]{2,1,0:T(8,128)(2,1)S(1)}, u32[]{:S(2)}, u32[]{:S(2)}) %all-to-all-start.9) | async-done | bytes 2621472 | tf_op jit(solution)/shard_map/all_to_all | solution.py:767
  467.5 5.2 %collective-permute-start.5 = (bf16[64,160,128]{2,1,0:T(8,128)(2,1)S(1)}, bf16[64,160,128]{2,1,0:T(8,128)(2,1)}, u32[]{:S(2)}, u32[]{:S(2)}) collective-permute-start(bf16[64,160,128]{2,1,0:T(8,128)(2,1)S(1)} %all-to-all-done.9.mine_ref), channel_id=1, source_target_pairs={{0,1},{1,0},{2,3},{3,2},{4,5},{5,4},{6,7},{7,6},{8,9},{9,8},{10,11... | collective-permute-start | bytes 7864328 | tf_op jit(solution)/shard_map/ppermute | solution.py:763
  486.1 6.4 %unpack.1 = (f32[768,768]{1,0:T(8,128)}, f32[768,768]{1,0:T(8,128)}, f32[768,768]{1,0:T(8,128)}, f32[768,768]{1,0:T(8,128)}, f32[24,768]{1,0:T(8,128)}) custom-call(s32[1]{0:T(128)} %bitcast.2.core_ref, bf16[64,160,128]{2,1,0:T(8,128)(2,1)} %copy-done.1, bf16[64,160,128]{2,1,0:T(8,128)(2,1)} %collective-permute-done.5.other_ref), custom_call_target="tpu_custom_call" | custom-call | flops 2359296 | bytes 14155776 | tf_op jit(solution)/shard_map/unpack/pallas_call | solution.py:748
  (145 shorter events, 77.9 us)
Async XLA Ops:
  10.4 10.0 %copy-start.30 = (s32[2,1,1]{0,2,1:T(1,128)S(1)}, s32[2,1,1]{0,2,1:T(1,128)}, u32[]{:S(2)}) copy-start(s32[2,1,1]{0,2,1:T(1,128)} %param.24) | copy-start | bytes 28
  10.4 10.5 %copy-start.24 = (bf16[2,768,2]{1,2,0:T(2,128)(2,1)S(1)}, bf16[2,768,2]{1,2,0:T(2,128)(2,1)}, u32[]{:S(2)}) copy-start(bf16[2,768,2]{1,2,0:T(2,128)(2,1)} %param.32) | copy-start | bytes 18436
  11.8 29.3 %all-to-all-start = ((bf16[16,64,768]{2,1,0:T(8,128)(2,1)}), bf16[16,64,768]{2,1,0:T(8,128)(2,1)}, u32[]{:S(2)}, u32[]{:S(2)}) async-start(bf16[16,64,768]{2,1,0:T(8,128)(2,1)} %broadcast_in_dim.66), calls=%async_computation | async-start | bytes 3145728 | tf_op jit(solution)/shard_map/all_to_all | solution.py:767
  42.4 42.6 %all-to-all-start.3 = ((bf16[16,64,768]{2,1,0:T(8,128)(2,1)}), bf16[16,64,768]{2,1,0:T(8,128)(2,1)}, u32[]{:S(2)}, u32[]{:S(2)}) async-start(bf16[16,64,768]{2,1,0:T(8,128)(2,1)} %broadcast_in_dim.70), calls=%async_computation.3 | async-start | bytes 3145728 | tf_op jit(solution)/shard_map/all_to_all | solution.py:767
  47.8 8.0 %copy-start.28 = (bf16[768]{0:T(1024)(128)(2,1)S(1)}, bf16[768]{0:T(1024)(128)(2,1)}, u32[]{:S(2)}) copy-start(bf16[768]{0:T(1024)(128)(2,1)} %param.30) | copy-start | bytes 4612
  47.8 8.9 %copy-start.22 = (bf16[768,12]{0,1:T(8,128)(2,1)S(1)}, bf16[768,12]{0,1:T(8,128)(2,1)}, u32[]{:S(2)}) copy-start(bf16[768,12]{0,1:T(8,128)(2,1)} %param.31) | copy-start | bytes 55300
  47.8 10.6 %copy-start.25 = (s32[2,1,1,192,2]{3,4,2,1,0:T(2,128)S(1)}, s32[2,1,1,192,2]{3,4,2,1,0:T(2,128)}, u32[]{:S(2)}) copy-start(s32[2,1,1,192,2]{3,4,2,1,0:T(2,128)} %param.22) | copy-start | bytes 9220
  47.8 11.4 %copy-start.26 = (s32[2,1,1,192,2]{3,4,2,1,0:T(2,128)S(1)}, s32[2,1,1,192,2]{3,4,2,1,0:T(2,128)}, u32[]{:S(2)}) copy-start(s32[2,1,1,192,2]{3,4,2,1,0:T(2,128)} %param.23) | copy-start | bytes 9220
  47.8 14.2 %collective-permute-start = (bf16[1024,768]{1,0:T(8,128)(2,1)}, bf16[1024,768]{1,0:T(8,128)(2,1)}, u32[]{:S(2)}, u32[]{:S(2)}) collective-permute-start(bf16[1024,768]{1,0:T(8,128)(2,1)} %bitcast.7.near_ref.refs_0_), channel_id=1, source_target_pairs={{0,1},{1,0},{2,3},{3,2},{4,5},{5,4},{6,7},{7,6},{8,9},{9,8},{10,11... | collective-permute-start | bytes 4718600 | tf_op jit(solution)/shard_map/ppermute | solution.py:763
  62.7 22.4 %copy-start.29 = (s32[2]{0:T(128)S(1)}, s32[2]{0:T(128)}, u32[]{:S(2)}) copy-start(s32[2]{0:T(128)} %add_bitcast_fusion) | copy-start | bytes 28
  62.7 22.5 %copy-start.18 = (s32[2,1,1,192,2]{4,3,0,2,1:T(8,128)S(1)}, s32[2,1,1,192,2]{4,3,0,2,1:T(8,128)}, u32[]{:S(2)}) copy-start(s32[2,1,1,192,2]{4,3,0,2,1:T(8,128)} %copy.52) | copy-start | bytes 9220
  62.7 22.5 %copy-start.19 = (s32[2,1,1,192,2]{4,3,0,2,1:T(8,128)S(1)}, s32[2,1,1,192,2]{4,3,0,2,1:T(8,128)}, u32[]{:S(2)}) copy-start(s32[2,1,1,192,2]{4,3,0,2,1:T(8,128)} %copy.51) | copy-start | bytes 9220
  62.7 24.7 %copy-start.17 = (bf16[768,12]{1,0:T(8,128)(2,1)S(1)}, bf16[768,12]{1,0:T(8,128)(2,1)}, u32[]{:S(2)}) copy-start(bf16[768,12]{1,0:T(8,128)(2,1)} %copy.49) | copy-start | bytes 55300
  85.0 16.7 %collective-permute-start.1 = (bf16[1024,768]{1,0:T(8,128)(2,1)}, bf16[1024,768]{1,0:T(8,128)(2,1)S(1)}, u32[]{:S(2)}, u32[]{:S(2)}) collective-permute-start(bf16[1024,768]{1,0:T(8,128)(2,1)} %bitcast.26.near_ref.refs_9_), channel_id=1, source_target_pairs={{0,1},{1,0},{2,3},{3,2},{4,5},{5,4},{6,7},{7,6},{8,9},{9,8},{10,11... | collective-permute-start | bytes 4718600 | tf_op jit(solution)/shard_map/ppermute | solution.py:763
  96.2 33.9 %all-to-all-start.1 = ((bf16[8,40,1536]{2,1,0:T(8,128)(2,1)}), bf16[8,40,1536]{2,1,0:T(8,128)(2,1)S(1)}, u32[]{:S(2)}, u32[]{:S(2)}) async-start(bf16[8,40,1536]{2,1,0:T(8,128)(2,1)} %bitcast.142), calls=%async_computation.1 | async-start | bytes 1966080 | tf_op jit(solution)/shard_map/all_to_all | solution.py:767
  125.0 10.0 %copy-start.23 = (bf16[768]{0:T(1024)(128)(2,1)S(1)}, bf16[768]{0:T(1024)(128)(2,1)}, u32[]{:S(2)}) copy-start(bf16[768]{0:T(1024)(128)(2,1)} %param.25) | copy-start | bytes 4612
  125.0 10.6 %copy-start.27 = (bf16[2,768]{1,0:T(2,128)(2,1)S(1)}, bf16[2,768]{1,0:T(2,128)(2,1)}, u32[]{:S(2)}) copy-start(bf16[2,768]{1,0:T(2,128)(2,1)} %param.33) | copy-start | bytes 9220
  130.1 6.1 %copy-start.15 = (bf16[8,40,1536]{2,1,0:T(8,128)(2,1)}, bf16[8,40,1536]{2,1,0:T(8,128)(2,1)S(1)}, u32[]{:S(2)}) copy-start(bf16[8,40,1536]{2,1,0:T(8,128)(2,1)S(1)} %all-to-all-done.1) | copy-start | bytes 2949124
  130.2 19.2 %all-to-all-start.4 = ((bf16[8,40,1536]{2,1,0:T(8,128)(2,1)}), bf16[8,40,1536]{2,1,0:T(8,128)(2,1)S(1)}, u32[]{:S(2)}, u32[]{:S(2)}) async-start(bf16[8,40,1536]{2,1,0:T(8,128)(2,1)} %bitcast.148), calls=%async_computation.4 | async-start | bytes 1966080 | tf_op jit(solution)/shard_map/all_to_all | solution.py:767
  149.4 30.0 %all-to-all-start.2 = ((bf16[8,40,1536]{2,1,0:T(8,128)(2,1)}), bf16[8,40,1536]{2,1,0:T(8,128)(2,1)S(1)}, u32[]{:S(2)}, u32[]{:S(2)}) async-start(bf16[8,40,1536]{2,1,0:T(8,128)(2,1)} %bitcast.147), calls=%async_computation.2 | async-start | bytes 1966080 | tf_op jit(solution)/shard_map/all_to_all | solution.py:767
  179.4 5.6 %copy-start.7 = (bf16[8,40,1536]{2,1,0:T(8,128)(2,1)}, bf16[8,40,1536]{2,1,0:T(8,128)(2,1)S(1)}, u32[]{:S(2)}) copy-start(bf16[8,40,1536]{2,1,0:T(8,128)(2,1)S(1)} %all-to-all-done.2) | copy-start | bytes 2949124
  179.4 55.2 %all-to-all-start.5 = ((bf16[8,40,1536]{2,1,0:T(8,128)(2,1)}), bf16[8,40,1536]{2,1,0:T(8,128)(2,1)S(1)}, u32[]{:S(2)}, u32[]{:S(2)}) async-start(bf16[8,40,1536]{2,1,0:T(8,128)(2,1)} %bitcast.34), calls=%async_computation.5 | async-start | bytes 1966080 | tf_op jit(solution)/shard_map/all_to_all | solution.py:767
  184.3 221.1 %all-reduce.7.cloned.1.call-start = ((), (), s32[]{:S(2)}) async-start(), calls=%async_computation.10 | async-start | bytes 18874368 | tf_op jit(solution)/shard_map/psum | solution.py:844
  234.3 79.5 %collective-permute-start.2 = (bf16[1024,768]{1,0:T(8,128)(2,1)}, bf16[1024,768]{1,0:T(8,128)(2,1)S(1)}, u32[]{:S(2)}, u32[]{:S(2)}) collective-permute-start(bf16[1024,768]{1,0:T(8,128)(2,1)} %get-tuple-element.134), channel_id=1, source_target_pairs={{0,1},{1,0},{2,3},{3,2},{4,5},{5,4},{6,7},{7,6},{8,9},{9,8},{10,11... | collective-permute-start | bytes 4718600 | tf_op jit(solution)/shard_map/ppermute | solution.py:763
  311.7 12.2 %collective-permute-start.4 = (bf16[64,160,128]{2,1,0:T(8,128)(2,1)}, bf16[64,160,128]{2,1,0:T(8,128)(2,1)}, u32[]{:S(2)}, u32[]{:S(2)}) collective-permute-start(bf16[64,160,128]{2,1,0:T(8,128)(2,1)} %get-tuple-element.154), channel_id=1, source_target_pairs={{0,1},{1,0},{2,3},{3,2},{4,5},{5,4},{6,7},{7,6},{8,9},{9,8},{10,11... | collective-permute-start | bytes 7864328 | tf_op jit(solution)/shard_map/ppermute | solution.py:763
  317.2 40.0 %all-to-all-start.6 = ((bf16[16,64,768]{2,1,0:T(8,128)(2,1)}), bf16[16,64,768]{2,1,0:T(8,128)(2,1)S(1)}, u32[]{:S(2)}, u32[]{:S(2)}) async-start(bf16[16,64,768]{2,1,0:T(8,128)(2,1)} %bitcast.134), calls=%async_computation.6 | async-start | bytes 3145728 | tf_op jit(solution)/shard_map/all_to_all | solution.py:767
  358.3 42.2 %all-to-all-start.8 = ((bf16[64,160,128]{2,1,0:T(8,128)(2,1)}), bf16[64,160,128]{2,1,0:T(8,128)(2,1)S(1)}, u32[]{:S(2)}, u32[]{:S(2)}) async-start(bf16[64,160,128]{2,1,0:T(8,128)(2,1)} %add_convert_fusion), calls=%async_computation.8 | async-start | bytes 5242880 | tf_op jit(solution)/shard_map/all_to_all | solution.py:767
  368.3 4.8 collective-permute-start.3
  400.5 23.5 %all-to-all-start.7 = ((bf16[16,64,768]{2,1,0:T(8,128)(2,1)}), bf16[16,64,768]{2,1,0:T(8,128)(2,1)}, u32[]{:S(2)}, u32[]{:S(2)}) async-start(bf16[16,64,768]{2,1,0:T(8,128)(2,1)} %bitcast.133), calls=%async_computation.7 | async-start | bytes 3145728 | tf_op jit(solution)/shard_map/all_to_all | solution.py:767
  425.9 41.6 %all-to-all-start.9 = ((bf16[64,160,128]{2,1,0:T(8,128)(2,1)}), bf16[64,160,128]{2,1,0:T(8,128)(2,1)S(1)}, u32[]{:S(2)}, u32[]{:S(2)}) async-start(bf16[64,160,128]{2,1,0:T(8,128)(2,1)} %broadcast_in_dim.75), calls=%async_computation.9 | async-start | bytes 5242880 | tf_op jit(solution)/shard_map/all_to_all | solution.py:767
  467.5 8.4 %copy-start.1 = (bf16[64,160,128]{2,1,0:T(8,128)(2,1)}, bf16[64,160,128]{2,1,0:T(8,128)(2,1)S(1)}, u32[]{:S(2)}) copy-start(bf16[64,160,128]{2,1,0:T(8,128)(2,1)S(1)} %all-to-all-done.9.mine_ref) | copy-start | bytes 7864324
  467.5 18.7 %collective-permute-start.5 = (bf16[64,160,128]{2,1,0:T(8,128)(2,1)S(1)}, bf16[64,160,128]{2,1,0:T(8,128)(2,1)}, u32[]{:S(2)}, u32[]{:S(2)}) collective-permute-start(bf16[64,160,128]{2,1,0:T(8,128)(2,1)S(1)} %all-to-all-done.9.mine_ref), channel_id=1, source_target_pairs={{0,1},{1,0},{2,3},{3,2},{4,5},{5,4},{6,7},{7,6},{8,9},{9,8},{10,11... | collective-permute-start | bytes 7864328 | tf_op jit(solution)/shard_map/ppermute | solution.py:763
  (16 other events, 50.3 us)
Sparse Core Ops, SparseCore 0:
  189.8 164.8 all-reduce.6
